TPU v7x, 256 devices: a whole 4x4x8 slice. The times are simulated.
256 devices in a mesh: replica: 8 (over z_lo, y), node: 32 (over x, z_hi, core).
Axes of the slice: x: 4, y: 4, z: 8 (z_hi: 4, z_lo: 2; z = z_hi * 2 + z_lo), core: 2. Of those that a mesh axis runs over, the one named last changes fastest.
Arguments:
- tokens: bfloat16 [65536, 6144], P(('replica', 'node')), may hold values from -6 to 6
- gain: float32 [6144], replicated, may hold values from 0.1 to 1.9
- w_up: bfloat16 [6144, 12288], P('replica', 'node'), may hold values from -0.078125 to 0.078125
- w_down: bfloat16 [12288, 6144], P('node', 'replica'), may hold values from -0.0546875 to 0.0546875
- cotangent: bfloat16 [65536, 6144], P(('replica', 'node')), may hold values from -2 to 2
- keep_index: int32 [32, 72], P('replica'), may hold values from 0 to 2047, as said below
Outputs:
- input_grad: bfloat16 [65536, 6144], P(('replica', 'node'))
- gain_grad: float32 [6144], replicated
- up_grad: bfloat16 [6144, 12288], P('replica', 'node')
- down_grad: bfloat16 [12288, 6144], P('node', 'replica')
Inputs may be any that keep to these rules, and one draw needn't show every extreme that they name: `keep_index`: in each sequence the kept positions are distinct and ascending. Each device's block of 256 tokens within a sequence holds at most 12 kept tokens, and exactly 12 on one of the 8 devices of every sequence.
All inputs are finite; a program needn't handle non-finite values.
Results may differ from a plain program's by a relative error of at most 0.024.
Values may be sent and summed in bfloat16 or wider, within the bound.
A program may use at most 128 MiB of HBM per device.

v0:
```python
import jax
import jax.numpy as jnp
from jax import lax
from jax.sharding import PartitionSpec as P

CAP = 12


epsilon = 1e-05


def gelu_tanh(values):
    return jax.nn.gelu(values, approximate=True)


def normalize(rows, gain):
    rows_f = rows.astype(jnp.float32)
    mean_val = jnp.mean(rows_f, axis=1, keepdims=True)
    centred = rows_f - mean_val
    variance = jnp.mean(centred * centred, axis=1, keepdims=True)
    rstd = lax.rsqrt(variance + epsilon)
    nhat = centred * rstd
    return ((nhat * gain).astype(jnp.bfloat16), nhat, rstd)


def local(tokens, gain, w_up, w_down, cotangent, keep_index):
    tok_dev = tokens.shape[0]
    nodes = lax.axis_size("node")
    my_index = lax.axis_index("node")
    seq_span = nodes // 4
    seq_len = tok_dev * seq_span
    seq_offsets = (jnp.arange(keep_index.shape[0], dtype=jnp.int32) * seq_len)[:, None]
    group_tok = (keep_index + seq_offsets).reshape(-1)
    total_rows = group_tok.shape[0]
    owner = group_tok // tok_dev
    before_me = jnp.sum((owner < my_index).astype(jnp.int32))
    my_count = jnp.sum((owner == my_index).astype(jnp.int32))
    slot_ids = jnp.arange(CAP, dtype=jnp.int32)
    live_slot = slot_ids < my_count
    pick_row = jnp.clip(before_me + slot_ids, 0, total_rows - 1)
    local_pos = jnp.where(live_slot, group_tok[pick_row] - my_index * tok_dev, 0)
    live_col = live_slot[:, None]
    own_x = jnp.where(live_col, tokens[local_pos], jnp.zeros((), jnp.bfloat16))
    own_dy = jnp.where(live_col, cotangent[local_pos], jnp.zeros((), jnp.bfloat16))
    up_full, down_full = (
        lax.all_gather(w_up, "replica", axis=0, tiled=True),
        lax.all_gather(w_down, "replica", axis=1, tiled=True),
    )
    rows_all, dy_all = (
        lax.all_gather(own_x, "node", axis=0, tiled=True),
        lax.all_gather(own_dy, "node", axis=0, tiled=True),
    )
    normed_all, nhat_all, rstd_all = normalize(rows_all, gain)
    own_nhat = lax.dynamic_slice_in_dim(nhat_all, my_index * CAP, CAP, 0)
    own_rstd = lax.dynamic_slice_in_dim(rstd_all, my_index * CAP, CAP, 0)
    pre_act = jnp.dot(normed_all, up_full, preferred_element_type=jnp.float32)
    act_f, back_fn = jax.vjp(gelu_tanh, pre_act)
    act = act_f.astype(jnp.bfloat16)
    d_act = lax.dot_general(
        dy_all, down_full, (((1,), (1,)), ((), ())), preferred_element_type=jnp.float32
    )
    d_pre = back_fn(d_act)[0].astype(jnp.bfloat16)
    d_norm_part = lax.dot_general(
        d_pre, up_full, (((1,), (1,)), ((), ())), preferred_element_type=jnp.float32
    )
    own_dnorm = lax.psum_scatter(
        d_norm_part.astype(jnp.bfloat16), "node", scatter_dimension=0, tiled=True
    ).astype(jnp.float32)
    scaled = own_dnorm * gain
    inner = (
        scaled
        - jnp.mean(scaled, axis=1, keepdims=True)
        - own_nhat * jnp.mean(scaled * own_nhat, axis=1, keepdims=True)
    )
    d_rows = jnp.where(live_col, own_rstd * inner, 0.0)
    gain_term = jnp.sum(jnp.where(live_col, own_dnorm * own_nhat, 0.0), axis=0)
    gain_grad = lax.psum(gain_term, ("replica", "node"))
    input_grad = cotangent.astype(jnp.float32).at[local_pos].add(d_rows).astype(jnp.bfloat16)
    up_grad = lax.psum_scatter(
        lax.dot_general(
            normed_all, d_pre, (((0,), (0,)), ((), ())), preferred_element_type=jnp.float32
        ).astype(jnp.bfloat16),
        "replica",
        scatter_dimension=0,
        tiled=True,
    )
    down_term = lax.dot_general(
        act, dy_all, (((0,), (0,)), ((), ())), preferred_element_type=jnp.float32
    )
    down_grad = lax.psum_scatter(
        down_term.astype(jnp.bfloat16), "replica", scatter_dimension=1, tiled=True
    )
    return (input_grad, gain_grad, up_grad, down_grad)


def solution(mesh):
    in_specs = (
        P(("replica", "node"), None),
        P(),
        P("replica", "node"),
        P("node", "replica"),
        P(("replica", "node"), None),
        P("replica", None),
    )
    out_specs = (P(("replica", "node"), None), P(), P("replica", "node"), P("node", "replica"))
    return jax.shard_map(local, mesh=mesh, in_specs=in_specs, out_specs=out_specs, check_vma=False)
```

profile of v0, /device:TPU:1, one launch (start us, length us, event | category | flops | bytes accessed | tf_op | source)
XLA Modules:
  0.0 622.8 jit_solution(9460221163447945073)
XLA Ops:
  11.5 3.1 gather_fusion.2
  18.3 71.2 %all-gather.11.cloned.1.call-done = bf16[32,12,6144]{2,1,0:T(8,128)(2,1)} async-done(((bf16[1,12,6144]{2,1,0:T(8,128)(2,1)}), bf16[32,12,6144]{2,1,0:T(8,128)(2,1)}) %all-gather.11.cloned.1.call-update) | async-done | bytes 4718608 | tf_op jit(solution)/shard_map/all_gather | solution.py:50
  89.4 3.9 convert_reduce_fusion
  93.5 8.5 %reshape.137 = f32[384,6144]{1,0:T(8,128)} reshape(bf16[32,12,6144]{2,1,0:T(8,128)(2,1)} %all-gather.11.cloned.1.call-done) | data formatting | bytes 14155776 | tf_op jit(solution)/shard_map/convert_element_type | solution.py:17
  101.9 57.6 %all-gather.13.cloned.1.call-done = bf16[32,12,6144]{2,1,0:T(8,128)(2,1)} async-done(((bf16[1,12,6144]{2,1,0:T(8,128)(2,1)}), bf16[32,12,6144]{2,1,0:T(8,128)(2,1)}) %all-gather.13.cloned.1.call-update) | async-done | bytes 4718608 | tf_op jit(solution)/shard_map/all_gather | solution.py:51
  159.5 7.6 %reshape.136 = bf16[384,6144]{1,0:T(8,128)(2,1)} reshape(bf16[32,12,6144]{2,1,0:T(8,128)(2,1)} %all-gather.13.cloned.1.call-done) | data formatting | bytes 9437184
  167.2 4.8 multiply_reduce_fusion
  172.0 47.1 %all-gather.7.cloned.1.call-done = bf16[384,6144]{1,0:T(8,128)(2,1)} async-done(((bf16[384,768]{1,0:T(8,128)(2,1)}), bf16[384,6144]{1,0:T(8,128)(2,1)}) %all-gather.7.cloned.1.call-update) | async-done | bytes 4718608 | tf_op jit(solution)/shard_map/all_gather | solution.py:47
  219.1 6.5 %fusion.41 = f32[384,384]{1,0:T(8,128)S(1)} fusion(bf16[384,6144]{1,0:T(8,128)(2,1)} %reshape.136, bf16[384,6144]{1,0:T(8,128)(2,1)} %all-gather.7.cloned.1.call-done), kind=kOutput, calls=%fused_computation.76 | convolution fusion | flops 1811939328 | bytes 10027008 | tf_op jit(solution)/shard_map/dot_general | solution.py:59
  225.6 9.2 %subtract_multiply_fusion = f32[384,6144]{1,0:T(8,128)} fusion(f32[384,6144]{1,0:T(8,128)} %reshape.137, f32[384]{0:T(512)S(1)} %add_rsqrt_fusion, f32[384]{0:T(512)S(1)} %reshape.140), kind=kLoop, calls=%fused_computation.6 | loop fusion | flops 4718592 | bytes 18877440 | tf_op jit(solution)/shard_map/mul | solution.py:22
  234.9 44.8 %all-gather.9.cloned.1.call-done = bf16[6144,384]{1,0:T(8,128)(2,1)} async-done(((bf16[768,384]{1,0:T(8,128)(2,1)}), bf16[6144,384]{1,0:T(8,128)(2,1)}) %all-gather.9.cloned.1.call-update) | async-done | bytes 4718608 | tf_op jit(solution)/shard_map/all_gather | solution.py:46
  279.7 6.9 %fusion.8 = (bf16[384,384]{1,0:T(8,128)(2,1)S(1)}, f32[384,384]{1,0:T(8,128)S(1)}) fusion(f32[384,384]{1,0:T(8,128)S(1)} %fusion.41, bf16[6144,384]{1,0:T(8,128)(2,1)} %all-gather.9.cloned.1.call-done, f32[384,6144]{1,0:T(8,128)} %subtract_multiply_fusion, f32[6144]{0:T(1024)S(1)} %copy-done.4), kind=kOutput, calls=%fused_computation.20 | convolution fusion | flops 1819607040 | bytes 15654912 | tf_op jit(solution)/shard_map/dot_general | solution.py:56
  286.6 7.2 %convolution_convert_fusion = bf16[384,6144]{1,0:T(8,128)(2,1)} fusion(bf16[384,6144]{1,0:T(8,128)(2,1)} %reshape.136, f32[384,384]{1,0:T(8,128)S(1)} %get-tuple-element.14), kind=kOutput, calls=%fused_computation.7 | convolution fusion | flops 1815625728 | bytes 10027008 | tf_op jit(solution)/shard_map/dot_general | solution.py:87
  294.0 8.9 %convolution_convert_fusion.1 = bf16[6144,384]{1,0:T(8,128)(2,1)} fusion(bf16[384,384]{1,0:T(8,128)(2,1)S(1)} %get-tuple-element.13, f32[384,6144]{1,0:T(8,128)} %subtract_multiply_fusion, f32[6144]{0:T(1024)S(1)} %copy-done.4), kind=kOutput, calls=%fused_computation.8 | convolution fusion | flops 1819017216 | bytes 14475264 | tf_op jit(solution)/shard_map/dot_general | solution.py:80
  302.9 7.9 %convolution_convert_fusion.2 = bf16[384,6144]{1,0:T(8,128)(2,1)} fusion(bf16[384,384]{1,0:T(8,128)(2,1)S(1)} %get-tuple-element.13, bf16[6144,384]{1,0:T(8,128)(2,1)} %all-gather.9.cloned.1.call-done), kind=kOutput, calls=%fused_computation.9 | convolution fusion | flops 1814298624 | bytes 9732096 | tf_op jit(solution)/shard_map/dot_general | solution.py:63
  310.8 133.1 %fusion = bf16[16,6144]{1,0:T(8,128)(2,1)S(1)} fusion(bf16[384,6144]{1,0:T(8,128)(2,1)} %convolution_convert_fusion.2), kind=kCustom, calls=%all-reduce-scatter | all-reduce-scatter fusion | flops 3145729 | bytes 4916224
  446.6 3.2 collective-permute-start.7
  449.9 2.6 collective-permute-start.4
  452.5 10.6 %collective-permute-start.3 = (bf16[16,6144]{1,0:T(8,128)(2,1)S(1)}, bf16[16,6144]{1,0:T(8,128)(2,1)}, u32[]{:S(2)}, u32[]{:S(2)}) collective-permute-start(bf16[16,6144]{1,0:T(8,128)(2,1)S(1)} %fusion), channel_id=1, source_target_pairs={{0,4},{1,5},{2,6},{3,7},{4,8},{5,9},{6,10},{7,11},{8,12},{9,13},{1... | collective-permute-start | bytes 589832
  463.1 2.8 collective-permute-start.2
  465.9 3.4 collective-permute-start.1
  469.3 2.1 collective-permute-start
  471.5 3.4 convert_element_type.38
  476.2 6.6 %collective-permute-done.3 = bf16[16,6144]{1,0:T(8,128)(2,1)} collective-permute-done((bf16[16,6144]{1,0:T(8,128)(2,1)S(1)}, bf16[16,6144]{1,0:T(8,128)(2,1)}, u32[]{:S(2)}, u32[]{:S(2)}) %collective-permute-start.3) | collective-permute-done | bytes 196640
  482.8 10.4 %collective-permute-done.2 = bf16[16,6144]{1,0:T(8,128)(2,1)} collective-permute-done((bf16[16,6144]{1,0:T(8,128)(2,1)S(1)}, bf16[16,6144]{1,0:T(8,128)(2,1)}, u32[]{:S(2)}, u32[]{:S(2)}) %collective-permute-start.2) | collective-permute-done | bytes 196640
  493.2 6.8 %collective-permute-done.1 = bf16[16,6144]{1,0:T(8,128)(2,1)} collective-permute-done((bf16[16,6144]{1,0:T(8,128)(2,1)S(1)}, bf16[16,6144]{1,0:T(8,128)(2,1)}, u32[]{:S(2)}, u32[]{:S(2)}) %collective-permute-start.1) | collective-permute-done | bytes 196640
  500.0 2.1 collective-permute-done
  502.1 20.9 %concatenate = bf16[140,6144]{1,0:T(8,128)(2,1)S(1)} concatenate(bf16[12,6144]{1,0:T(8,128)(2,1)} %copy-done.7, bf16[16,6144]{1,0:T(8,128)(2,1)} %copy-done.5, bf16[16,6144]{1,0:T(8,128)(2,1)} %copy-done.6, bf16[16,6144]{1,0:T(8,128)(2,1)} %collective-permute-done.4, bf16[16,6144]{1,0:T(8,128)(2,1)} %collective-permute-done.3, bf16[16,6144]{1,0:T(8,128)(2,1)} %collective-permute-done.2, ...), dimensions={0} | concatenate | bytes 3440640
  524.1 1.4 fusion.19
  525.6 7.3 %scatter_custom_fusion = f32[256,6144]{1,0:T(8,128)} fusion(f32[256,6144]{1,0:T(8,128)} %convert_element_type.38, s32[12]{0:T(128)S(1)} %fusion.36, f32[384,6144]{1,0:T(8,128)} %subtract_multiply_fusion, s32[]{:T(128)S(6)} %select_n.63, s32[]{:T(128)} %constant.15.clone.1, f32[]{:T(128)} %constant.48.clone.1, f32[12]{0:T(128)S(1)} %get-tuple-element.15, ...), kind=kCustom, calls=%fused_computation.30 | custom fusion | flops 589824 | bytes 6913032 | tf_op jit(solution)/shard_map/scatter-add | solution.py:78
  532.9 4.9 convert_element_type.46
  537.7 78.2 %psum.7 = f32[6144]{0:T(1024)} all-reduce(f32[6144]{0:T(1024)S(1)} %get-tuple-element.4), channel_id=1, replica_groups=mesh['replica'=8,'node'=32] {'replica','node'}, use_global_device_ids=true, to_apply=%region_9.10 | all-reduce | flops 6144 | bytes 49152 | tf_op jit(solution)/shard_map/psum | solution.py:77
  (57 shorter events, 12.8 us)
Async XLA Ops:
  7.2 7.5 %copy-start = (bf16[256,6144]{1,0:T(8,128)(2,1)S(1)}, bf16[256,6144]{1,0:T(8,128)(2,1)}, u32[]{:S(2)}) copy-start(bf16[256,6144]{1,0:T(8,128)(2,1)} %param.6) | copy-start | bytes 9437188
  7.2 82.3 %all-gather.11.cloned.1.call-start = ((), (), s32[]{:S(2)}) async-start(), calls=%async_computation.6 | async-start | bytes 6488064 | tf_op jit(solution)/shard_map/all_gather | solution.py:50
  16.1 143.4 %all-gather.13.cloned.1.call-start = ((), (), s32[]{:S(2)}) async-start(), calls=%async_computation.7 | async-start | bytes 6488064 | tf_op jit(solution)/shard_map/all_gather | solution.py:51
  16.9 202.2 %all-gather.7.cloned.1.call-start = ((), (), s32[]{:S(2)}) async-start(), calls=%async_computation.2 | async-start | bytes 5308416 | tf_op jit(solution)/shard_map/all_gather | solution.py:47
  17.6 262.0 %all-gather.9.cloned.1.call-start = ((), (), s32[]{:S(2)}) async-start(), calls=%async_computation.3 | async-start | bytes 5308416 | tf_op jit(solution)/shard_map/all_gather | solution.py:46
  18.2 597.7 %reduce-scatter.7.cloned.1.call-start = ((), (), s32[]{:S(2)}) async-start(), calls=%async_computation.5 | async-start | bytes 5308416 | tf_op jit(solution)/shard_map/reduce_scatter | solution.py:90
  225.6 54.1 %copy-start.4 = (f32[6144]{0:T(1024)S(1)}, f32[6144]{0:T(1024)}, u32[]{:S(2)}) copy-start(f32[6144]{0:T(1024)} %param.7) | copy-start | bytes 73732
  293.8 322.1 %reduce-scatter.5.cloned.1.call-start = ((), (), s32[]{:S(2)}) async-start(), calls=%async_computation.4 | async-start | bytes 5308416 | tf_op jit(solution)/shard_map/reduce_scatter | solution.py:79
  310.8 160.6 %copy-start.2 = (bf16[256,6144]{1,0:T(8,128)(2,1)S(1)}, bf16[256,6144]{1,0:T(8,128)(2,1)}, u32[]{:S(2)}) copy-start(bf16[256,6144]{1,0:T(8,128)(2,1)} %param.10) | copy-start | bytes 9437188
  443.9 22.0 %collective-permute-start.6 = (bf16[16,6144]{1,0:T(8,128)(2,1)S(1)}, bf16[16,6144]{1,0:T(8,128)(2,1)S(1)}, u32[]{:S(2)}, u32[]{:S(2)}) collective-permute-start(bf16[16,6144]{1,0:T(8,128)(2,1)S(1)} %fusion), channel_id=1, source_target_pairs={{0,7},{1,8},{2,9},{3,10},{4,11},{5,12},{6,13},{7,14},{8,15},{9,16}... | collective-permute-start | bytes 589832
  445.3 24.1 %collective-permute-start.5 = (bf16[16,6144]{1,0:T(8,128)(2,1)S(1)}, bf16[16,6144]{1,0:T(8,128)(2,1)S(1)}, u32[]{:S(2)}, u32[]{:S(2)}) collective-permute-start(bf16[16,6144]{1,0:T(8,128)(2,1)S(1)} %fusion), channel_id=1, source_target_pairs={{0,6},{1,7},{2,8},{3,9},{4,10},{5,11},{6,12},{7,13},{8,14},{9,15},... | collective-permute-start | bytes 589832
  446.6 16.5 %collective-permute-start.7 = (bf16[12,6144]{1,0:T(8,128)(2,1)S(1)}, bf16[12,6144]{1,0:T(8,128)(2,1)S(1)}, u32[]{:S(2)}, u32[]{:S(2)}) collective-permute-start(bf16[12,6144]{1,0:T(8,128)(2,1)S(1)} %slice.6), channel_id=1, source_target_pairs={{0,8},{1,9},{2,10},{3,11},{4,12},{5,13},{6,14},{7,15},{8,16},{9,17... | collective-permute-start | bytes 442376
  449.9 26.3 %collective-permute-start.4 = (bf16[16,6144]{1,0:T(8,128)(2,1)S(1)}, bf16[16,6144]{1,0:T(8,128)(2,1)}, u32[]{:S(2)}, u32[]{:S(2)}) collective-permute-start(bf16[16,6144]{1,0:T(8,128)(2,1)S(1)} %fusion), channel_id=1, source_target_pairs={{0,5},{1,6},{2,7},{3,8},{4,9},{5,10},{6,11},{7,12},{8,13},{9,14},{... | collective-permute-start | bytes 589832
  452.5 30.3 %collective-permute-start.3 = (bf16[16,6144]{1,0:T(8,128)(2,1)S(1)}, bf16[16,6144]{1,0:T(8,128)(2,1)}, u32[]{:S(2)}, u32[]{:S(2)}) collective-permute-start(bf16[16,6144]{1,0:T(8,128)(2,1)S(1)} %fusion), channel_id=1, source_target_pairs={{0,4},{1,5},{2,6},{3,7},{4,8},{5,9},{6,10},{7,11},{8,12},{9,13},{1... | collective-permute-start | bytes 589832
  463.1 8.3 %copy-start.7 = (bf16[12,6144]{1,0:T(8,128)(2,1)}, bf16[12,6144]{1,0:T(8,128)(2,1)S(1)}, u32[]{:S(2)}) copy-start(bf16[12,6144]{1,0:T(8,128)(2,1)S(1)} %collective-permute-done.7) | copy-start | bytes 442372
  463.1 30.1 %collective-permute-start.2 = (bf16[16,6144]{1,0:T(8,128)(2,1)S(1)}, bf16[16,6144]{1,0:T(8,128)(2,1)}, u32[]{:S(2)}, u32[]{:S(2)}) collective-permute-start(bf16[16,6144]{1,0:T(8,128)(2,1)S(1)} %fusion), channel_id=1, source_target_pairs={{0,3},{1,4},{2,5},{3,6},{4,7},{5,8},{6,9},{7,10},{8,11},{9,12},{10... | collective-permute-start | bytes 589832
  465.9 3.4 copy-start.5
  465.9 34.0 %collective-permute-start.1 = (bf16[16,6144]{1,0:T(8,128)(2,1)S(1)}, bf16[16,6144]{1,0:T(8,128)(2,1)}, u32[]{:S(2)}, u32[]{:S(2)}) collective-permute-start(bf16[16,6144]{1,0:T(8,128)(2,1)S(1)} %fusion), channel_id=1, source_target_pairs={{0,2},{1,3},{2,4},{3,5},{4,6},{5,7},{6,8},{7,9},{8,10},{9,11},{10,... | collective-permute-start | bytes 589832
  469.3 2.1 copy-start.6
  469.3 32.7 %collective-permute-start = (bf16[16,6144]{1,0:T(8,128)(2,1)S(1)}, bf16[16,6144]{1,0:T(8,128)(2,1)}, u32[]{:S(2)}, u32[]{:S(2)}) collective-permute-start(bf16[16,6144]{1,0:T(8,128)(2,1)S(1)} %fusion), channel_id=1, source_target_pairs={{0,1},{1,2},{2,3},{3,4},{4,5},{5,6},{6,7},{7,8},{8,9},{9,10},{10,1... | collective-permute-start | bytes 589832
  471.4 3.4 copy-start.8
  522.9 1.2 copy-start.3
  525.6 90.3 %copy-start.1 = (bf16[256,6144]{1,0:T(8,128)(2,1)S(1)}, bf16[256,6144]{1,0:T(8,128)(2,1)}, u32[]{:S(2)}) copy-start(bf16[256,6144]{1,0:T(8,128)(2,1)} %param.6) | copy-start | bytes 9437188
Sparse Core Ops, SparseCore 0:
  16.3 73.1 all-gather.10
  92.6 66.9 all-gather.12
  161.3 57.7 all-gather.6
  220.8 58.8 all-gather.8
  293.9 93.2 reduce-scatter.6
  390.2 111.0 reduce-scatter.4
where the time goes:
time: 625 us; the launch traced here: 623 us
  waiting for transfers between devices  249 us (40%)
  blocking collectives  211 us (34%)
  local copies, waits for them, and re-layouts  43.5 us (7%)
  other arithmetic  39.3 us (6%)
  matrix products  37.3 us (6%)
  starting transfers between devices  27.8 us (4%)
  between operations  15 us (2%)
    unnamed x1, blocking collectives  133 us
    psum x1, blocking collectives, local(): gain_grad = lax.psum(gain_term, ('replica', 'node'))  78.2 us
    all_gather x1, waiting for transfers between devices, local(): lax.all_gather(own_x, 'node', axis=0, tiled=True)  71.2 us
    all_gather x1, waiting for transfers between devices, local(): lax.all_gather(own_dy, 'node', axis=0, tiled=True)  57.6 us
    all_gather x1, waiting for transfers between devices, local(): lax.all_gather(w_down, 'replica', axis=1, tiled=True)  47.1 us
    all_gather x1, waiting for transfers between devices, local(): lax.all_gather(w_up, 'replica', axis=0, tiled=True)  44.8 us
    unnamed x22, local copies, waits for them, and re-layouts  30.4 us
    unnamed x14, waiting for transfers between devices  27.8 us
  transfers between devices with their start and end apart: 14, of which 8 were waited for; matrix products, arithmetic and copies ran while one was open for 37% of the time, Pallas kernels for 0%

commit v1 on v0

v1 whole, which is shorter than its diff:
```python
import functools

import jax
import jax.numpy as jnp
from jax import lax
from jax.experimental import pallas as pl
from jax.experimental.pallas import tpu as pltpu
from jax.sharding import PartitionSpec as P

CAP = 12
TOK = 256
D = 6144
HALF = 3072
QW = 768
FB = 384
SEQ_ROWS = 72
BOTH = 144
EPS = 1e-05
NONE = 255
F32 = jnp.float32
BF16 = jnp.bfloat16
MESH = pl.DeviceIdType.MESH

A_TANH = 0.7978845608028654
B_TANH = 0.044715


def dot(a, b, ca=1, cb=0):
    return lax.dot_general(a, b, (((ca,), (cb,)), ((), ())), preferred_element_type=F32)


def iota(shape, dim):
    return lax.broadcasted_iota(jnp.int32, shape, dim)


def body(
    keep_ref, tok_ref, cot_ref, gain_ref, wup_ref, wdn_ref,
    rows_ref, sel_ref, gsum_ref, upg_ref, dng_ref,
    pk0, pk1, g0, g1, ordered, t_buf, wu, wd, keepf, psend, precv, ad, act_t, dpre_t, dpre_b,
    csend, crecv, cown, xs1, xr1, xs2, xr2, zs, zr, nhat_s, dy_s, rstd_s,
    ys1, yr1, ys2, yr2, ykeep, gx, gz, gy,
    ssem, rsem,
):
    r = lax.axis_index("replica")
    n = lax.axis_index("node")
    zl, y = r // 4, lax.rem(r, 4)
    x, zh, c = n // 8, lax.rem(n // 2, 4), lax.rem(n, 2)

    def dev(x_=None, y_=None, zh_=None, zl_=None, c_=None):
        x_ = x if x_ is None else x_
        y_ = y if y_ is None else y_
        zh_ = zh if zh_ is None else zh_
        zl_ = zl if zl_ is None else zl_
        c_ = c if c_ is None else c_
        return (zl_ * 4 + y_, x_ * 8 + zh_ * 2 + c_)

    def step(v, d):
        return lax.rem(v + (d % 4), 4)

    count = [0]
    started = []

    def send(src, dst, to):
        k = count[0]
        count[0] += 1
        d = pltpu.make_async_remote_copy(
            src_ref=src, dst_ref=dst, send_sem=ssem.at[k], recv_sem=rsem.at[k],
            device_id=to, device_id_type=MESH,
        )
        d.start()
        started.append(d)
        return d

    z_peers = [(a, b, e) for a in range(4) for b in range(2) for e in range(2)][1:]

    def z_peer(a, b, e):
        return dev(zh_=step(zh, a), zl_=lax.rem(zl + b, 2), c_=lax.rem(c + e, 2))

    barrier = pltpu.get_barrier_semaphore()
    peers = [z_peer(*p) for p in z_peers]
    peers += [dev(x_=step(x, d)) for d in (1, 2, 3)]
    peers += [dev(y_=step(y, d)) for d in (1, 2, 3)]
    for p in peers:
        pl.semaphore_signal(barrier, inc=1, device_id=p, device_id_type=MESH)

    n8 = lax.rem(n, 8)
    kv = keep_ref[pl.ds(x, 1), :]
    owner = kv // TOK
    before = jnp.sum((owner < n8).astype(F32), axis=1, keepdims=True)
    mine = jnp.sum((owner == n8).astype(F32), axis=1, keepdims=True)
    slot_col = iota((16, SEQ_ROWS), 0).astype(F32)
    j_row = iota((16, SEQ_ROWS), 1).astype(F32)
    local_pos = (kv - n8 * TOK).astype(F32)
    hit = (j_row == before + slot_col) & (slot_col < mine)
    pos = jnp.sum(jnp.where(hit, local_pos, 0.0), axis=1, keepdims=True)
    live = iota((16, TOK), 0).astype(F32) < mine
    sel = jnp.where((iota((16, TOK), 1).astype(F32) == pos) & live, 1.0, 0.0).astype(BF16)
    sel_ref[...] = sel

    row_i, lane_i = iota((16, 128), 0), iota((16, 128), 1)
    kind = lax.rem(row_i, 8)
    i_in = lane_i - (zh * 2 + c) * 16
    slot = jnp.where(
        kind == 0, i_in,
        jnp.where(kind == 1, i_in - 8, jnp.where(kind < 6, 8 + i_in - 4 * (kind - 2), i_in)),
    )
    is_b = (kind >= 2) & (kind < 6)
    ok = (slot >= jnp.where(is_b, 8, 0)) & (slot < jnp.where(kind < 2, 8, CAP))
    slot_f = slot.astype(F32)
    target = jnp.where(ok & (slot_f < mine), before + slot_f, float(NONE))
    here = (i_in >= 0) & (i_in < 16) & (row_i // 8 == zl)
    meta = jnp.where(here, target, 0.0).astype(BF16)

    xr = dot(sel, tok_ref[...])
    dyr = dot(sel, cot_ref[...])
    mean = jnp.mean(xr, axis=1, keepdims=True)
    cen = xr - mean
    rstd = lax.rsqrt(jnp.mean(cen * cen, axis=1, keepdims=True) + EPS)
    nhat = cen * rstd
    nhat_s[...] = nhat
    dy_s[...] = dyr
    rstd_s[...] = jnp.broadcast_to(rstd, (16, 128))
    normed = nhat * gain_ref[...]

    def pack(rows, col):
        blk = rows[:, col:col + 1536]
        main = jnp.concatenate([blk[0:8, 0:768], blk[0:8, 768:1536]], axis=0)
        t = [blk[8:16, 384 * b:384 * (b + 1)] for b in range(4)]
        extra = jnp.concatenate(
            [t[0] + pltpu.roll(t[1], 4, 0), t[2] + pltpu.roll(t[3], 4, 0)], axis=0
        )
        return main.astype(BF16), extra.astype(BF16)

    for a, rows in enumerate((normed, dyr)):
        for h in range(2):
            m, e = pack(rows, h * HALF)
            pk0[a, h, :, 0:768] = m
            pk0[a, h, :, 768:1152] = e
            pk0[a, h, :, 1152:1280] = meta
            m, e = pack(rows, h * HALF + 1536)
            pk1[a, h, :, 0:768] = m
            pk1[a, h, :, 768:1152] = e
    wu[pl.ds(y, 1)] = wup_ref[...][None]
    wd[pl.ds(y, 1)] = wdn_ref[...][None]

    pl.semaphore_wait(barrier, len(peers))

    pks, gs = (pk0, pk1), (g0, g1)
    first = []
    for k in range(2):
        group = []
        for b, e in ((0, 1), (1, 0), (1, 1)):
            zl2, c2 = lax.rem(zl + b, 2), lax.rem(c + e, 2)
            group.append(
                send(pks[k].at[c2, zl2], gs[k].at[zl, zh, c], dev(zl_=zl2, c_=c2))
            )
        first.append(group)

    wu_r = send(wup_ref, wu.at[y], dev(y_=step(y, 1)))
    wd_l = send(wdn_ref, wd.at[y], dev(y_=step(y, -1)))
    wu_l = send(wup_ref, wu.at[y], dev(y_=step(y, -1)))
    wd_r = send(wdn_ref, wd.at[y], dev(y_=step(y, 1)))

    for k in range(2):
        gs[k][pl.ds(zl, 1), pl.ds(zh, 1), pl.ds(c, 1)] = pks[k][pl.ds(c, 1), pl.ds(zl, 1)][None]

    up_z, dn_z = dev(zh_=step(zh, 1)), dev(zh_=step(zh, -1))
    ring = []
    for k in range(2):
        for d in first[k]:
            d.wait_recv()
        ring.append(
            (send(gs[k].at[:, zh], gs[k].at[:, zh], up_z),
             send(gs[k].at[:, zh], gs[k].at[:, zh], dn_z))
        )
    ring2 = []
    for k in range(2):
        ring[k][0].wait_recv()
        f0 = send(gs[k].at[:, step(zh, -1), 0], gs[k].at[:, step(zh, -1), 0], up_z)
        ring[k][1].wait_recv()
        f1 = send(gs[k].at[:, step(zh, 1), 1], gs[k].at[:, step(zh, 1), 1], dn_z)
        ring2.append((f0, f1))

    xp, xm, sib = dev(x_=step(x, 1)), dev(x_=step(x, -1)), dev(c_=1 - c)
    row_f = iota((BOTH, 128), 0).astype(F32)

    def one_hot(meta_sum, kk):
        return jnp.concatenate(
            [
                jnp.where(row_f == meta_sum[kk:kk + 1, :], 1.0, 0.0),
                jnp.where(row_f == meta_sum[8 + kk:9 + kk, :] + SEQ_ROWS, 1.0, 0.0),
            ],
            axis=1,
        )

    hops = []
    for k in range(2):
        for d in ring2[k]:
            d.wait_recv()
        if k == 0:
            ms = jnp.zeros((16, 128), F32)
            for a in range(2):
                for b in range(4):
                    for e in range(2):
                        ms = ms + g0[a, b, e, :, 1152:1280].astype(F32)
            oh = [one_hot(ms, kk).astype(BF16) for kk in range(6)]
            oh_slot = one_hot(ms, 6)
        ga = gs[k][:, :, :, :, 0:768].reshape(256, 768)
        gb = gs[k][:, :, :, :, 768:1152].reshape(256, 384)
        for b in range(4):
            cols = slice((b % 2) * 384, (b % 2) * 384 + 384)
            v = dot(oh[b // 2], ga[:, cols]) + dot(oh[2 + b], gb)
            ordered[2 * k + b // 2, :, cols] = v.astype(BF16)
        src, dst = ordered.at[pl.ds(2 * k, 2)], t_buf.at[c, x, pl.ds(2 * k, 2)]
        hops.append((send(src, dst, xp), send(src, dst, xm), send(src, dst, sib)))
        t_buf[pl.ds(c, 1), pl.ds(x, 1), 2 * k:2 * k + 2] = ordered[2 * k:2 * k + 2][None, None]

    wu_r.wait_recv()
    wu_f = send(wu.at[step(y, -1)], wu.at[step(y, -1)], dev(y_=step(y, 1)))
    wd_l.wait_recv()
    wd_f = send(wd.at[step(y, 1)], wd.at[step(y, 1)], dev(y_=step(y, -1)))

    def piece_of(s, k):
        return t_buf.at[c, s, pl.ds(2 * k, 2)]

    s_m, s_p, s_2 = step(x, -1), step(x, 1), step(x, 2)
    hops[0][0].wait_recv()
    p = piece_of(s_m, 0)
    fx0 = send(p, p, xp)
    sib_m0 = send(p, p, sib)
    hops[0][1].wait_recv()
    p = piece_of(s_p, 0)
    sib_p0 = send(p, p, sib)
    hops[1][1].wait_recv()
    p = piece_of(s_p, 1)
    fx1 = send(p, p, xm)
    sib_p1 = send(p, p, sib)
    hops[1][0].wait_recv()
    p = piece_of(s_m, 1)
    sib_m1 = send(p, p, sib)

    wu_l.wait_recv()
    wd_r.wait_recv()
    wu_f.wait_recv()
    wd_f.wait_recv()

    zp = dev(zl_=1 - zl)

    def forward_part(s):
        pre = jnp.zeros((BOTH, FB), F32)
        dac = jnp.zeros((BOTH, FB), F32)
        for q in range(4):
            pre = pre + dot(t_buf[0, s, q], wu[q])
            dac = dac + dot(t_buf[1, s, q], wd[q], 1, 1)
        lo = jnp.concatenate([pre[:SEQ_ROWS], dac[:SEQ_ROWS]], axis=0)
        hi = jnp.concatenate([pre[SEQ_ROWS:], dac[SEQ_ROWS:]], axis=0)
        is0 = zl == 0
        keepf[s] = jnp.where(is0, lo, hi)
        psend[s] = jnp.where(is0, hi, lo).astype(BF16)
        return send(psend.at[s], precv.at[s], zp)

    def middle(s):
        full = keepf[s] + precv[s].astype(F32)
        v, da = full[:SEQ_ROWS], full[SEQ_ROWS:]
        v2 = v * v
        t = jnp.tanh(A_TANH * (v + B_TANH * v * v2))
        act = 0.5 * v * (1.0 + t)
        slope = 0.5 * (1.0 + t) + 0.5 * v * (1.0 - t * t) * (A_TANH * (1.0 + 3.0 * B_TANH * v2))
        both = jnp.concatenate([act, da * slope], axis=0).astype(BF16)
        ad[zl, s] = both
        return send(ad.at[zl, s], ad.at[zl, s], zp)

    parts = {}
    hops[0][2].wait_recv()
    hops[1][2].wait_recv()
    parts[0] = forward_part(x)
    sib_m0.wait_recv()
    sib_m1.wait_recv()
    parts[1] = forward_part(s_m)
    sib_p0.wait_recv()
    sib_p1.wait_recv()
    parts[2] = forward_part(s_p)
    fx0.wait_recv()
    p = piece_of(s_2, 0)
    sib_20 = send(p, p, sib)
    fx1.wait_recv()
    p = piece_of(s_2, 1)
    sib_21 = send(p, p, sib)
    mids = []
    for i, s in ((0, x), (1, s_m), (2, s_p)):
        parts[i].wait_recv()
        mids.append(middle(s))
    sib_20.wait_recv()
    sib_21.wait_recv()
    parts[3] = forward_part(s_2)
    parts[3].wait_recv()
    mids.append(middle(s_2))

    for m in mids:
        m.wait_recv()
    a_all, d_all = [], []
    for s in range(4):
        u, w = ad[0, s].astype(F32), ad[1, s].astype(F32)
        a_all += [u[:SEQ_ROWS], w[:SEQ_ROWS]]
        d_s = jnp.concatenate([u[SEQ_ROWS:], w[SEQ_ROWS:]], axis=0)
        d_all.append(d_s)
        dpre_b[s] = d_s.astype(BF16)
    act_t[...] = jnp.concatenate(a_all, axis=0).T.astype(BF16)
    dpre_t[...] = jnp.concatenate(d_all, axis=0).T.astype(BF16)

    gx[pl.ds(x, 1)] = jnp.zeros((1, 8, QW), F32)

    def norm_part(s):
        for j in range(2):
            q_own, q_oth = 2 * c + j, 2 * (1 - c) + j
            for q, mine_ in ((q_oth, False), (q_own, True)):
                v = dot(dpre_b[s], wu[q], 1, 1)
                if mine_:
                    cown[s, j] = v
                else:
                    csend[s, j] = v.astype(BF16)
                g = jnp.sum(v * t_buf[0, s, q].astype(F32), axis=0, keepdims=True)
                gx[pl.ds(x, 1), pl.ds(q, 1)] += g[None]
        return send(csend.at[s], crecv.at[s], sib)

    cores = {}
    for i, s in ((2, s_2), (1, s_p), (-1, s_m), (0, x)):
        cores[i] = norm_part(s)
    gain1 = []
    for d in (1, 2, 3):
        gain1.append(send(gx.at[x], gx.at[x], dev(x_=step(x, d))))

    def up_part(q):
        return dot(dpre_t[...], t_buf[0, :, q].reshape(4 * BOTH, QW))

    def down_part(q):
        return dot(act_t[...], t_buf[1, :, q].reshape(4 * BOTH, QW))

    yp, ym = dev(y_=step(y, 1)), dev(y_=step(y, -1))
    q_p, q_m, q_2 = step(y, 1), step(y, -1), step(y, 2)
    ys1[0] = up_part(q_2).astype(BF16)
    y1u = send(ys1.at[0], yr1.at[0], yp)
    ys1[1] = down_part(q_2).astype(BF16)
    y1d = send(ys1.at[1], yr1.at[1], ym)

    def summed(s, j):
        return cown[s, j] + crecv[s, j].astype(F32)

    cores[2].wait_recv()
    xs1[0] = summed(s_2, 0).astype(BF16)
    x1p = send(xs1.at[0], xr1.at[0], xp)
    xs1[1] = summed(s_2, 1).astype(BF16)
    x1m = send(xs1.at[1], xr1.at[1], xm)

    ys2[0, 1] = down_part(q_p).astype(BF16)
    y2pd = send(ys2.at[0, 1], yr2.at[0, 1], yp)
    ys2[1, 0] = up_part(q_m).astype(BF16)
    y2mu = send(ys2.at[1, 0], yr2.at[1, 0], ym)

    cores[1].wait_recv()
    xs2[0, 1] = summed(s_p, 1).astype(BF16)
    x2p1 = send(xs2.at[0, 1], xr2.at[0, 1], xp)
    cores[-1].wait_recv()
    xs2[1, 0] = summed(s_m, 0).astype(BF16)
    x2m0 = send(xs2.at[1, 0], xr2.at[1, 0], xm)

    ykeep[0] = up_part(q_p)
    ykeep[1] = down_part(q_m)

    x1p.wait_recv()
    xs2[0, 0] = (summed(s_p, 0) + xr1[0].astype(F32)).astype(BF16)
    x2p0 = send(xs2.at[0, 0], xr2.at[0, 0], xp)
    x1m.wait_recv()
    xs2[1, 1] = (summed(s_m, 1) + xr1[1].astype(F32)).astype(BF16)
    x2m1 = send(xs2.at[1, 1], xr2.at[1, 1], xm)

    for d in gain1:
        d.wait_recv()
    slot_me = zh * 2 + c
    gz[pl.ds(zl, 1), pl.ds(slot_me, 1)] = (gx[0] + gx[1] + gx[2] + gx[3])[None, None]
    gain2 = [send(gz.at[zl, slot_me], gz.at[zl, slot_me], z_peer(*p_)) for p_ in z_peers]

    y1u.wait_recv()
    ys2[0, 0] = (ykeep[0] + yr1[0].astype(F32)).astype(BF16)
    y2pu = send(ys2.at[0, 0], yr2.at[0, 0], yp)
    y1d.wait_recv()
    ys2[1, 1] = (ykeep[1] + yr1[1].astype(F32)).astype(BF16)
    y2md = send(ys2.at[1, 1], yr2.at[1, 1], ym)

    ykeep[0] = up_part(y)
    ykeep[1] = down_part(y)

    cores[0].wait_recv()
    for d in (x2p0, x2p1, x2m0, x2m1):
        d.wait_recv()
    oh_s = oh_slot.T.astype(BF16)
    for j in range(2):
        total = summed(x, j) + xr2[0, j].astype(F32) + xr2[1, j].astype(F32)
        v = dot(oh_s, total.astype(BF16)).astype(BF16)
        zs[:, :, :, :, 768 * j:768 * (j + 1)] = v.reshape(2, 4, 2, 16, 768)
    owners = []
    for a, b, e in z_peers:
        zh2, zl2, c2 = step(zh, a), lax.rem(zl + b, 2), lax.rem(c + e, 2)
        owners.append(send(zs.at[zl2, zh2, c2], zr.at[zl, c, zh], z_peer(a, b, e)))
    zr[pl.ds(zl, 1), pl.ds(c, 1), pl.ds(zh, 1)] = zs[pl.ds(zl, 1), pl.ds(zh, 1), pl.ds(c, 1)].reshape(1, 1, 1, 16, 1536)

    for d in gain2:
        d.wait_recv()
    for h in range(2):
        g = gz[h, 0]
        for i in range(1, 8):
            g = g + gz[h, i]
        gy[pl.ds(y, 1), h] = g[None]
    gain3 = [send(gy.at[y], gy.at[y], dev(y_=step(y, d))) for d in (1, 2, 3)]

    for d in owners:
        d.wait_recv()
    cols = []
    for a in range(2):
        for e in range(2):
            t = zr[a, e, 0].astype(F32)
            for b in range(1, 4):
                t = t + zr[a, e, b].astype(F32)
            cols.append(t)
    d_norm = jnp.concatenate(cols, axis=1)
    h = d_norm * gain_ref[...]
    nh = nhat_s[...]
    inner = h - jnp.mean(h, axis=1, keepdims=True) - nh * jnp.mean(h * nh, axis=1, keepdims=True)
    rows_ref[...] = (dy_s[...] + rstd_s[:, 0:1] * inner).astype(BF16)

    for d in gain3:
        d.wait_recv()
    gsum_ref[...] = gy[0] + gy[1] + gy[2] + gy[3]

    for d in (y2pd, y2mu, y2pu, y2md):
        d.wait_recv()
    upg_ref[...] = (ykeep[0] + yr2[0, 0].astype(F32) + yr2[1, 0].astype(F32)).astype(BF16)
    dng_ref[...] = (ykeep[1] + yr2[0, 1].astype(F32) + yr2[1, 1].astype(F32)).astype(BF16)

    for d in started:
        d.wait_send()


N_COPIES = 96


def kernel_call(keep, tokens, cotangent, gain, w_up, w_down):
    vmem = pl.BlockSpec(memory_space=pltpu.VMEM)

    def v(shape, dt=BF16):
        return pltpu.VMEM(shape, dt)

    scratch = [
        v((2, 2, 16, 1280)), v((2, 2, 16, 1152)),
        v((2, 4, 2, 16, 1280)), v((2, 4, 2, 16, 1152)),
        v((4, BOTH, QW)), v((2, 4, 4, BOTH, QW)),
        v((4, QW, FB)), v((4, FB, QW)),
        v((4, BOTH, FB), F32), v((4, BOTH, FB)), v((4, BOTH, FB)),
        v((2, 4, BOTH, FB)),
        v((FB, 4 * BOTH)), v((FB, 4 * BOTH)), v((4, BOTH, FB)),
        v((4, 2, BOTH, QW)), v((4, 2, BOTH, QW)), v((4, 2, BOTH, QW), F32),
        v((2, BOTH, QW)), v((2, BOTH, QW)), v((2, 2, BOTH, QW)), v((2, 2, BOTH, QW)),
        v((2, 4, 2, 16, 1536)), v((2, 2, 4, 16, 1536)),
        v((16, D), F32), v((16, D), F32), v((16, 128), F32),
        v((2, FB, QW)), v((2, FB, QW)), v((2, 2, FB, QW)), v((2, 2, FB, QW)),
        v((2, FB, QW), F32),
        v((4, 8, QW), F32), v((2, 8, 8, QW), F32), v((4, 2, 8, QW), F32),
        pltpu.SemaphoreType.DMA((N_COPIES,)), pltpu.SemaphoreType.DMA((N_COPIES,)),
    ]
    return pl.pallas_call(
        body,
        out_shape=(
            jax.ShapeDtypeStruct((16, D), BF16),
            jax.ShapeDtypeStruct((16, TOK), BF16),
            jax.ShapeDtypeStruct((2, 8, QW), F32),
            jax.ShapeDtypeStruct((FB, QW), BF16),
            jax.ShapeDtypeStruct((FB, QW), BF16),
        ),
        in_specs=[vmem] * 6,
        out_specs=(vmem,) * 5,
        scratch_shapes=scratch,
        compiler_params=pltpu.CompilerParams(
            collective_id=0, has_side_effects=True, vmem_limit_bytes=60 * 2**20
        ),
    )(keep, tokens, cotangent, gain, w_up, w_down)


def local(tokens, gain, w_up, w_down, cotangent, keep_index):
    rows, sel, gsum, up_t, down = kernel_call(
        keep_index, tokens, cotangent, gain.reshape(1, D), w_up, w_down
    )
    placed = dot(sel, rows, 0, 0).astype(BF16)
    kept = jnp.sum(sel.astype(F32), axis=0)[:, None] > 0.5
    input_grad = jnp.where(kept, placed, cotangent)
    gain_grad = gsum[:, :4].reshape(D) / gain
    return (input_grad, gain_grad, up_t.T, down)


def solution(mesh):
    in_specs = (
        P(("replica", "node"), None),
        P(),
        P("replica", "node"),
        P("node", "replica"),
        P(("replica", "node"), None),
        P("replica", None),
    )
    out_specs = (P(("replica", "node"), None), P(), P("replica", "node"), P("node", "replica"))
    return jax.shard_map(local, mesh=mesh, in_specs=in_specs, out_specs=out_specs, check_vma=False)
```

time: 625 us -> 142 us (0.23)
  waiting for transfers between devices: 249 us -> 0 us
  blocking collectives: 211 us -> 0 us
  Pallas kernels: 0 us -> 131 us
  local copies, waits for them, and re-layouts: 43.5 us -> 3.76 us
  other arithmetic: 39.3 us -> 1.34 us
  matrix products: 37.3 us -> 3.68 us
  starting transfers between devices: 27.8 us -> 0 us
  between operations: 15 us -> 0.67 us
    all_gather x4 -> x0, waiting for transfers between devices: 221 us -> none  [the longest x1 71.2 us: local(): lax.all_gather(own_x, 'node', axis=0, tiled=True)]
    unnamed x1 -> x0, blocking collectives: 133 us -> none
    pallas_call x0 -> x1, Pallas kernels: none -> 131 us  [kernel_call(): pl.pallas_call(body, out_shape=(jax.ShapeDtypeStruct((16, D), BF16), jax....]
    psum x1 -> x0, blocking collectives: 78.2 us -> none  [local(): gain_grad = lax.psum(gain_term, ('replica', 'node'))]
    dot_general x5 -> x1, matrix products: 37.3 us -> 3.68 us  [dot(): lax.dot_general(a, b, (((ca,), (cb,)), ((), ())), preferred_element_type=...]
    unnamed x14 -> x0, waiting for transfers between devices: 27.8 us -> none
    unnamed x22 -> x8, local copies, waits for them, and re-layouts: 30.4 us -> 2.94 us
    unnamed x8 -> x0, starting transfers between devices: 27.4 us -> none
  transfers between devices with their start and end apart: 14 -> 0, of which waited for: 8 -> 0; matrix products, arithmetic and copies ran while one was open for 37% -> 0% of each run, Pallas kernels for 0% -> 0%
where the time goes in v1:
time: 142 us; the launch traced here: 140 us
  Pallas kernels  131 us (92%)
  local copies, waits for them, and re-layouts  3.76 us (3%)
  matrix products  3.68 us (3%)
    pallas_call x1, Pallas kernels, kernel_call(): pl.pallas_call(body, out_shape=(jax.ShapeDtypeStruct((16, D), BF16), jax....  131 us
    dot_general x1, matrix products, dot(): lax.dot_general(a, b, (((ca,), (cb,)), ((), ())), preferred_element_type=...  3.68 us
    unnamed x8, local copies, waits for them, and re-layouts  2.94 us

profile of v1, /device:TPU:1, one launch (start us, length us, event | category | flops | bytes accessed | tf_op | source)
XLA Modules:
  0.0 140.2 jit_solution(9518567446684187382)
XLA Ops:
  0.6 0.0 copy-start.2
  0.6 0.0 copy-start
  0.7 130.7 %shard_map.93 = (bf16[16,6144]{1,0:T(8,128)(2,1)}, bf16[16,256]{1,0:T(8,128)(2,1)}, f32[2,8,768]{2,1,0:T(8,128)}, bf16[384,768]{1,0:T(8,128)(2,1)}, bf16[384,768]{1,0:T(8,128)(2,1)}) custom-call(s32[4,72]{1,0:T(4,128)} %keep_ref.1, bf16[256,6144]{1,0:T(8,128)(2,1)} %tok_ref.1, bf16[256,6144]{1,0:T(8,128)(2,1)} %cot_ref.1, f32[1,6144]{1,0:T(1,128)} %bitcast.5, ...), custom_call_target="tpu_custom_call" | custom-call | tf_op jit(solution)/shard_map/pallas_call | solution.py:470
  131.4 0.7 convert_reduce_fusion
  132.1 0.8 slice.3
  132.9 0.0 copy-done.2
  132.9 0.6 div.3
  133.5 2.1 %copy.10 = bf16[768,384]{1,0:T(8,128)(2,1)} copy(bf16[768,384]{0,1:T(8,128)(2,1)} %bitcast.4) | data formatting | bytes 1179648
  135.7 0.0 copy-done
  135.7 0.0 copy-start.1
  135.7 3.7 %fusion = bf16[256,6144]{1,0:T(8,128)(2,1)} fusion(bf16[256,6144]{1,0:T(8,128)(2,1)S(1)} %copy-done, bf16[16,256]{1,0:T(8,128)(2,1)} %get-tuple-element.9, bf16[16,6144]{1,0:T(8,128)(2,1)} %get-tuple-element.10, pred[256]{0:T(512)(128)(4,1)S(1)} %broadcast_compare_fusion), kind=kOutput, calls=%fused_computation.1 | convolution fusion | flops 53477376 | bytes 6496512 | tf_op jit(solution)/shard_map/dot_general | solution.py:29
  139.3 0.0 copy-done.1
  139.3 0.8 copy.12
  (2 shorter events, 0.0 us)
Async XLA Ops:
  0.6 132.3 %copy-start.2 = (f32[6144]{0:T(1024)S(1)}, f32[6144]{0:T(1024)}, u32[]{:S(2)}) copy-start(f32[6144]{0:T(1024)} %param.7) | copy-start | bytes 73732
  0.6 135.0 %copy-start = (bf16[256,6144]{1,0:T(8,128)(2,1)S(1)}, bf16[256,6144]{1,0:T(8,128)(2,1)}, u32[]{:S(2)}) copy-start(bf16[256,6144]{1,0:T(8,128)(2,1)} %cot_ref.1) | copy-start | bytes 9437188
  135.7 3.7 %copy-start.1 = (bf16[384,768]{1,0:T(8,128)(2,1)S(1)}, bf16[384,768]{1,0:T(8,128)(2,1)}, u32[]{:S(2)}) copy-start(bf16[384,768]{1,0:T(8,128)(2,1)} %get-tuple-element.25) | copy-start | bytes 1769476

commit v2 on v1

v2 whole, which is shorter than its diff:
```python
import functools

import jax
import jax.numpy as jnp
from jax import lax
from jax.experimental import pallas as pl
from jax.experimental.pallas import tpu as pltpu
from jax.sharding import PartitionSpec as P

CAP = 12
TOK = 256
D = 6144
HALF = 3072
QW = 768
CW = 512
CHUNKS = 6
WW = 512
FB = 384
SEQ_ROWS = 72
BOTH = 144
EPS = 1e-05
NONE = 255
F32 = jnp.float32
BF16 = jnp.bfloat16
MESH = pl.DeviceIdType.MESH

A_TANH = 0.7978845608028654
B_TANH = 0.044715


def dot(a, b, ca=1, cb=0):
    return lax.dot_general(a, b, (((ca,), (cb,)), ((), ())), preferred_element_type=F32)


def iota(shape, dim):
    return lax.broadcasted_iota(jnp.int32, shape, dim)


def body(
    keep_ref, gain_ref, tok_hbm, cot_hbm, wup_ref, wdn_ref,
    rows_ref, sel_ref, gout_ref, upg_ref, dng_ref,
    tok_ref, cot_ref, pk0, pkn, g0, gn, ordered, t_buf, wu, wd,
    keepf, psend, precv, act_t, dpre_t, act_b, dpre_b,
    csend, crecv, cown, xs1, xr1, xs2, xr2, zs, zr, nhat_s, dy_s, rstd_s,
    ys1, yr1, ys2, yr2, ykeep, gx, gz, gy,
    ssem, rsem, lsem,
):
    r = lax.axis_index("replica")
    n = lax.axis_index("node")
    zl, y = r // 4, lax.rem(r, 4)
    x, zh, c = n // 8, lax.rem(n // 2, 4), lax.rem(n, 2)

    def dev(x_=None, y_=None, zh_=None, zl_=None, c_=None):
        x_ = x if x_ is None else x_
        y_ = y if y_ is None else y_
        zh_ = zh if zh_ is None else zh_
        zl_ = zl if zl_ is None else zl_
        c_ = c if c_ is None else c_
        return (zl_ * 4 + y_, x_ * 8 + zh_ * 2 + c_)

    def step(v, d):
        return lax.rem(v + (d % 4), 4)

    count = [0]
    started = []

    def send(src, dst, to):
        k = count[0]
        count[0] += 1
        d = pltpu.make_async_remote_copy(
            src_ref=src, dst_ref=dst, send_sem=ssem.at[k], recv_sem=rsem.at[k],
            device_id=to, device_id_type=MESH,
        )
        d.start()
        started.append(d)
        return d

    def fetch(src, dst, k):
        d = pltpu.make_async_copy(src, dst, lsem.at[k])
        d.start()
        return d

    def col_of(ref, first, width):
        return ref.at[:, pl.ds(pl.multiple_of(first, 128), width)]

    z_peers = [(a, b, e) for a in range(4) for b in range(2) for e in range(2)][1:]

    def z_peer(a, b, e):
        return dev(zh_=step(zh, a), zl_=lax.rem(zl + b, 2), c_=lax.rem(c + e, 2))

    barrier = pltpu.get_barrier_semaphore()
    peers = [z_peer(*p) for p in z_peers]
    peers += [dev(x_=step(x, d)) for d in (1, 2, 3)]
    peers += [dev(y_=step(y, d)) for d in (1, 2, 3)]
    for p in peers:
        pl.semaphore_signal(barrier, inc=1, device_id=p, device_id_type=MESH)
    tok_in = fetch(tok_hbm, tok_ref, 0)
    cot_in = fetch(cot_hbm, cot_ref, 1)
    wu_own = wu.at[pl.ds(pl.multiple_of(y * QW, QW), QW)]
    wd_own = col_of(wd, y * QW, QW)
    wu_in = fetch(wup_ref, wu_own, 2)
    wd_in = fetch(wdn_ref, wd_own, 3)

    n8 = lax.rem(n, 8)
    kv = keep_ref[pl.ds(x, 1), :]
    owner = kv // TOK
    before = jnp.sum((owner < n8).astype(F32), axis=1, keepdims=True)
    mine = jnp.sum((owner == n8).astype(F32), axis=1, keepdims=True)
    slot_col = iota((16, SEQ_ROWS), 0).astype(F32)
    j_row = iota((16, SEQ_ROWS), 1).astype(F32)
    local_pos = (kv - n8 * TOK).astype(F32)
    hit = (j_row == before + slot_col) & (slot_col < mine)
    pos = jnp.sum(jnp.where(hit, local_pos, 0.0), axis=1, keepdims=True)
    live = iota((16, TOK), 0).astype(F32) < mine
    sel = jnp.where((iota((16, TOK), 1).astype(F32) == pos) & live, 1.0, 0.0).astype(BF16)
    sel_ref[...] = sel.astype(F32).T.astype(BF16)

    row_i, lane_i = iota((16, 128), 0), iota((16, 128), 1)
    kind = lax.rem(row_i, 8)
    i_in = lane_i - (zh * 2 + c) * 16
    slot = jnp.where(
        kind == 0, i_in,
        jnp.where(kind == 1, i_in - 8, jnp.where(kind < 6, 8 + i_in - 4 * (kind - 2), i_in)),
    )
    is_b = (kind >= 2) & (kind < 6)
    ok = (slot >= jnp.where(is_b, 8, 0)) & (slot < jnp.where(kind < 2, 8, CAP))
    slot_f = slot.astype(F32)
    target = jnp.where(ok & (slot_f < mine), before + slot_f, float(NONE))
    here = (i_in >= 0) & (i_in < 16) & (row_i // 8 == zl)
    meta = jnp.where(here, target, 0.0).astype(BF16)

    pks = [pk0] + [pkn.at[k] for k in range(CHUNKS - 1)]
    gs = [g0] + [gn.at[k] for k in range(CHUNKS - 1)]

    def pack(rows, a):
        for h in range(2):
            for k in range(CHUNKS):
                col = h * HALF + k * CW
                blk = rows[:, col:col + CW]
                main = jnp.concatenate([blk[0:8, 0:256], blk[0:8, 256:512]], axis=0)
                t = [blk[8:16, 128 * b:128 * (b + 1)] for b in range(4)]
                extra = jnp.concatenate(
                    [t[0] + pltpu.roll(t[1], 4, 0), t[2] + pltpu.roll(t[3], 4, 0)], axis=0
                )
                pks[k][a, h, :, 0:256] = main.astype(BF16)
                pks[k][a, h, :, 256:384] = extra.astype(BF16)
            pk0[a, h, :, 384:512] = meta

    tok_in.wait()
    xr = dot(sel, tok_ref[...])
    mean = jnp.mean(xr, axis=1, keepdims=True)
    cen = xr - mean
    rstd = lax.rsqrt(jnp.mean(cen * cen, axis=1, keepdims=True) + EPS)
    nhat = cen * rstd
    nhat_s[...] = nhat
    rstd_s[...] = jnp.broadcast_to(rstd, (16, 128))
    pack(nhat * gain_ref[...], 0)
    cot_in.wait()
    dyr = dot(sel, cot_ref[...])
    dy_s[...] = dyr
    pack(dyr, 1)

    pl.semaphore_wait(barrier, len(peers))

    first = []
    for k in range(CHUNKS):
        group = []
        for b, e in ((0, 1), (1, 0), (1, 1)):
            zl2, c2 = lax.rem(zl + b, 2), lax.rem(c + e, 2)
            group.append(
                send(pks[k].at[c2, zl2], gs[k].at[zl, zh, c], dev(zl_=zl2, c_=c2))
            )
        first.append(group)

    wu_in.wait()
    wd_in.wait()
    wu_r = send(wu_own, wu_own, dev(y_=step(y, 1)))
    wd_l = send(wd_own, wd_own, dev(y_=step(y, -1)))
    wu_l = send(wu_own, wu_own, dev(y_=step(y, -1)))
    wd_r = send(wd_own, wd_own, dev(y_=step(y, 1)))

    for k in range(CHUNKS):
        gs[k][pl.ds(zl, 1), pl.ds(zh, 1), pl.ds(c, 1)] = pks[k][pl.ds(c, 1), pl.ds(zl, 1)][None]

    up_z, dn_z = dev(zh_=step(zh, 1)), dev(zh_=step(zh, -1))
    xp, xm, sib = dev(x_=step(x, 1)), dev(x_=step(x, -1)), dev(c_=1 - c)
    s_m, s_p, s_2 = step(x, -1), step(x, 1), step(x, 2)
    row_f = iota((BOTH, 128), 0).astype(F32)
    ring, ring2, hops = {}, {}, {}
    oh = []

    def z_own(k):
        for d in first[k]:
            d.wait_recv()
        ring[k] = (
            send(gs[k].at[:, zh], gs[k].at[:, zh], up_z),
            send(gs[k].at[:, zh], gs[k].at[:, zh], dn_z),
        )

    def z_next(k):
        ring[k][0].wait_recv()
        f0 = send(gs[k].at[:, step(zh, -1), 0], gs[k].at[:, step(zh, -1), 0], up_z)
        ring[k][1].wait_recv()
        f1 = send(gs[k].at[:, step(zh, 1), 1], gs[k].at[:, step(zh, 1), 1], dn_z)
        ring2[k] = (f0, f1)

    def one_hot(meta_sum, kk):
        return jnp.concatenate(
            [
                jnp.where(row_f == meta_sum[kk:kk + 1, :], 1.0, 0.0),
                jnp.where(row_f == meta_sum[8 + kk:9 + kk, :] + SEQ_ROWS, 1.0, 0.0),
            ],
            axis=1,
        )

    def chunk_of(a, s, k):
        return t_buf.at[a, s, :, pl.ds(k * CW, CW)]

    def order(k):
        for d in ring2[k]:
            d.wait_recv()
        if k == 0:
            ms = jnp.zeros((16, 128), F32)
            for a in range(2):
                for b in range(4):
                    for e in range(2):
                        ms = ms + g0[a, b, e, :, 384:512].astype(F32)
            oh.extend(one_hot(ms, kk).astype(BF16) for kk in range(6))
            oh.append(one_hot(ms, 6))
        ga = gs[k][:, :, :, :, 0:256].reshape(256, 256)
        gb = gs[k][:, :, :, :, 256:384].reshape(256, 128)
        for a in range(2):
            v = dot(oh[a], ga) + jnp.concatenate(
                [dot(oh[2 + 2 * a], gb), dot(oh[3 + 2 * a], gb)], axis=1
            )
            ordered[k, :, 256 * a:256 * (a + 1)] = v.astype(BF16)
        dst = chunk_of(c, x, k)
        hops[k] = (send(ordered.at[k], dst, xp), send(ordered.at[k], dst, xm))
        t_buf[pl.ds(c, 1), pl.ds(x, 1), :, CW * k:CW * (k + 1)] = ordered[k][None, None]
        if k % 2:
            to_sib(0, x, k // 2)

    sibs, fx = {}, {}

    def to_sib(i, s, pair):
        p = t_buf.at[c, s, :, pl.ds(2 * CW * pair, 2 * CW)]
        sibs[i, pair] = send(p, p, sib)

    def pass_on(k):
        hops[k][0].wait_recv()
        hops[k][1].wait_recv()
        p = chunk_of(c, s_p if k % 2 else s_m, k)
        fx[k] = send(p, p, xm if k % 2 else xp)
        if k % 2:
            to_sib(-1, s_m, k // 2)
            to_sib(1, s_p, k // 2)

    z_own(0)
    z_own(1)
    z_next(0)
    z_own(2)
    z_next(1)
    order(0)
    z_own(3)
    z_next(2)
    order(1)
    z_own(4)
    z_next(3)
    order(2)
    z_own(5)
    z_next(4)
    pass_on(0)
    order(3)
    z_next(5)
    pass_on(1)
    order(4)
    pass_on(2)
    order(5)

    def wu_at(y_):
        return wu.at[pl.ds(pl.multiple_of(y_ * QW, QW), QW)]

    wu_r.wait_recv()
    p = wu_at(step(y, -1))
    wu_f = send(p, p, dev(y_=step(y, 1)))
    wd_l.wait_recv()
    p = col_of(wd, step(y, 1) * QW, QW)
    wd_f = send(p, p, dev(y_=step(y, -1)))

    for k in range(3, CHUNKS):
        pass_on(k)

    for d in (wu_l, wd_r, wu_f, wd_f):
        d.wait_recv()

    zp = dev(zl_=1 - zl)

    def forward_part(i, s):
        pre = dot(t_buf[0, s], wu[...])
        dac = dot(t_buf[1, s], wd[...], 1, 1)
        keepf[i, 0] = pre
        keepf[i, 1] = dac
        psend[i, 0] = pre.astype(BF16)
        psend[i, 1] = dac.astype(BF16)
        parts[i] = send(psend.at[i], precv.at[i], zp)

    def middle(i, s):
        parts[i].wait_recv()
        v = keepf[i, 0] + precv[i, 0].astype(F32)
        da = keepf[i, 1] + precv[i, 1].astype(F32)
        v2 = v * v
        t = jnp.tanh(A_TANH * (v + B_TANH * v * v2))
        act = 0.5 * v * (1.0 + t)
        slope = 0.5 * (1.0 + t) + 0.5 * v * (1.0 - t * t) * (A_TANH * (1.0 + 3.0 * B_TANH * v2))
        act_b[s] = act.astype(BF16)
        dpre_b[s] = (da * slope).astype(BF16)

    parts = {}

    def from_sib(i):
        for k in range(3):
            sibs[i, k].wait_recv()

    def far_pair(k):
        fx[2 * k].wait_recv()
        fx[2 * k + 1].wait_recv()
        to_sib(2, s_2, k)

    from_sib(0)
    forward_part(0, x)
    far_pair(0)
    from_sib(-1)
    forward_part(1, s_m)
    far_pair(1)
    from_sib(1)
    forward_part(2, s_p)
    middle(0, x)
    far_pair(2)
    middle(1, s_m)
    from_sib(2)
    forward_part(3, s_2)
    middle(2, s_p)
    middle(3, s_2)

    dpre_t[...] = dpre_b[...].reshape(4 * BOTH, FB).astype(F32).T.astype(BF16)
    act_t[...] = act_b[...].reshape(4 * BOTH, FB).astype(F32).T.astype(BF16)

    def rows_of(a, q):
        v = t_buf[a, :, :, pl.ds(pl.multiple_of(q * QW, 128), QW)]
        return v.reshape(4 * BOTH, QW)

    def up_part(q):
        return dot(dpre_t[...], rows_of(0, q))

    def down_part(q):
        return dot(act_t[...], rows_of(1, q))

    yp, ym = dev(y_=step(y, 1)), dev(y_=step(y, -1))
    q_p, q_m, q_2 = step(y, 1), step(y, -1), step(y, 2)
    ys1[0] = up_part(q_2).astype(BF16)
    y1u = send(ys1.at[0], yr1.at[0], yp)
    ys1[1] = down_part(q_2).astype(BF16)
    y1d = send(ys1.at[1], yr1.at[1], ym)

    gx[pl.ds(x, 1)] = jnp.zeros((1, 8, WW), F32)
    cores, x1, x2, own = {}, {}, {}, {}

    def norm_wave(w):
        for cc, mine_ in ((1 - c, False), (c, True)):
            first_col = cc * (3 * WW) + w * WW
            wt = wu[pl.ds(pl.multiple_of(first_col, WW), WW), :]
            g = jnp.zeros((1, WW), F32)
            for s in range(4):
                v = dot(dpre_b[s], wt, 1, 1)
                if mine_:
                    cown[w, s] = v
                else:
                    csend[w, s] = v.astype(BF16)
                rows = t_buf[0, s, :, pl.ds(pl.multiple_of(first_col, WW), WW)]
                g = g + jnp.sum(v * rows.astype(F32), axis=0, keepdims=True)
            gx[pl.ds(x, 1), pl.ds(cc * 3 + w, 1)] = g[None]
            if not mine_:
                cores[w] = send(csend.at[w], crecv.at[w], sib)

    def summed(w, s, lo, hi):
        return cown[w, s, :, lo:hi] + crecv[w, s, :, lo:hi].astype(F32)

    def x_first(w):
        cores[w].wait_recv()
        xs1[w, 0] = summed(w, s_2, 0, 256).astype(BF16)
        a = send(xs1.at[w, 0], xr1.at[w, 0], xp)
        xs1[w, 1] = summed(w, s_2, 256, 512).astype(BF16)
        x1[w] = (a, send(xs1.at[w, 1], xr1.at[w, 1], xm))

    def x_second(w):
        xs2[w, 0, :, 256:512] = summed(w, s_p, 256, 512).astype(BF16)
        xs2[w, 1, :, 0:256] = summed(w, s_m, 0, 256).astype(BF16)
        x1[w][0].wait_recv()
        xs2[w, 0, :, 0:256] = (summed(w, s_p, 0, 256) + xr1[w, 0].astype(F32)).astype(BF16)
        a = send(xs2.at[w, 0], xr2.at[w, 0], xp)
        x1[w][1].wait_recv()
        xs2[w, 1, :, 256:512] = (summed(w, s_m, 256, 512) + xr1[w, 1].astype(F32)).astype(BF16)
        x2[w] = (a, send(xs2.at[w, 1], xr2.at[w, 1], xm))

    owners = {}

    def to_owners(w):
        for d in x2[w]:
            d.wait_recv()
        total = summed(w, x, 0, WW) + xr2[w, 0].astype(F32) + xr2[w, 1].astype(F32)
        total = total.astype(BF16)
        v = dot(own[0], total[:, 0:256]) + dot(own[1], total[:, 256:512])
        zs[w, :, :, :, :, 0:256] = v.astype(BF16).reshape(2, 4, 2, 16, 256)
        v = dot(own[2], total[:, 0:128])
        for b in range(1, 4):
            v = v + dot(own[2 + b], total[:, 128 * b:128 * (b + 1)])
        zs[w, :, :, :, :, 256:384] = v.astype(BF16).reshape(2, 4, 2, 16, 128)
        owners[w] = []
        for a, b, e in z_peers:
            zh2, zl2, c2 = step(zh, a), lax.rem(zl + b, 2), lax.rem(c + e, 2)
            owners[w].append(send(zs.at[w, zl2, zh2, c2], zr.at[w, zl, c, zh], z_peer(a, b, e)))
        zr[w, pl.ds(zl, 1), pl.ds(c, 1), pl.ds(zh, 1)] = zs[
            w, pl.ds(zl, 1), pl.ds(zh, 1), pl.ds(c, 1)
        ].reshape(1, 1, 1, 16, 384)

    for kk in range(6):
        own[kk] = oh[kk].astype(F32).T.astype(BF16)

    norm_wave(0)
    norm_wave(1)
    x_first(0)
    norm_wave(2)
    gain1 = [send(gx.at[x], gx.at[x], dev(x_=step(x, d))) for d in (1, 2, 3)]

    ys2[0, 1] = down_part(q_p).astype(BF16)
    y2pd = send(ys2.at[0, 1], yr2.at[0, 1], yp)
    x_first(1)
    ys2[1, 0] = up_part(q_m).astype(BF16)
    y2mu = send(ys2.at[1, 0], yr2.at[1, 0], ym)
    x_second(0)
    x_first(2)
    ykeep[0] = up_part(q_p)
    x_second(1)
    ykeep[1] = down_part(q_m)

    y1u.wait_recv()
    ys2[0, 0] = (ykeep[0] + yr1[0].astype(F32)).astype(BF16)
    y2pu = send(ys2.at[0, 0], yr2.at[0, 0], yp)
    y1d.wait_recv()
    ys2[1, 1] = (ykeep[1] + yr1[1].astype(F32)).astype(BF16)
    y2md = send(ys2.at[1, 1], yr2.at[1, 1], ym)

    to_owners(0)
    x_second(2)
    ykeep[0] = up_part(y)
    ykeep[1] = down_part(y)
    to_owners(1)

    for d in gain1:
        d.wait_recv()
    slot_me = zh * 2 + c
    gz[pl.ds(zl, 1), pl.ds(slot_me, 1)] = (gx[0] + gx[1] + gx[2] + gx[3])[None, None]
    gain2 = [send(gz.at[zl, slot_me], gz.at[zl, slot_me], z_peer(*p_)) for p_ in z_peers]
    to_owners(2)

    for d in gain2:
        d.wait_recv()
    for h in range(2):
        g = gz[h, 0]
        for i in range(1, 8):
            g = g + gz[h, i]
        gy[pl.ds(y, 1), h] = g[None]
    gain3 = [send(gy.at[y], gy.at[y], dev(y_=step(y, d))) for d in (1, 2, 3)]

    cols = []
    for w in range(3):
        for d in owners[w]:
            d.wait_recv()
    zero4 = iota((8, 128), 0) < 4
    for a in range(2):
        for e in range(2):
            for w in range(3):
                t = zr[w, a, e, 0].astype(F32)
                for b in range(1, 4):
                    t = t + zr[w, a, e, b].astype(F32)
                top = jnp.concatenate([t[0:8, 0:256], t[8:16, 0:256]], axis=1)
                e0, e1 = t[0:8, 256:384], t[8:16, 256:384]
                low = [e0, pltpu.roll(e0, 4, 0), e1, pltpu.roll(e1, 4, 0)]
                low = jnp.concatenate([jnp.where(zero4, v, 0.0) for v in low], axis=1)
                cols.append(jnp.concatenate([top, low], axis=0))
    d_norm = jnp.concatenate(cols, axis=1)
    h = d_norm * gain_ref[...]
    nh = nhat_s[...]
    inner = h - jnp.mean(h, axis=1, keepdims=True) - nh * jnp.mean(h * nh, axis=1, keepdims=True)
    rows_ref[...] = (dy_s[...] + rstd_s[:, 0:1] * inner).astype(BF16)

    for d in gain3:
        d.wait_recv()
    for h in range(2):
        g = gy[0, h] + gy[1, h] + gy[2, h] + gy[3, h]
        for i in range(6):
            at = slice(h * HALF + i * WW, h * HALF + (i + 1) * WW)
            gout_ref[:, at] = g[i:i + 1, :] / gain_ref[:, at]

    for d in (y2pd, y2mu, y2pu, y2md):
        d.wait_recv()
    dng_ref[...] = (ykeep[1] + yr2[0, 1].astype(F32) + yr2[1, 1].astype(F32)).astype(BF16)
    upg_ref[...] = (ykeep[0] + yr2[0, 0].astype(F32) + yr2[1, 0].astype(F32)).T.astype(BF16)

    for d in started:
        d.wait_send()


N_COPIES = 192


def kernel_call(keep, tokens, cotangent, gain, w_up, w_down):
    vmem = pl.BlockSpec(memory_space=pltpu.VMEM)
    hbm = pl.BlockSpec(memory_space=pl.ANY)

    def v(shape, dt=BF16):
        return pltpu.VMEM(shape, dt)

    scratch = [
        v((TOK, D)), v((TOK, D)),
        v((2, 2, 16, 512)), v((CHUNKS - 1, 2, 2, 16, 384)),
        v((2, 4, 2, 16, 512)), v((CHUNKS - 1, 2, 4, 2, 16, 384)),
        v((CHUNKS, BOTH, CW)), v((2, 4, BOTH, HALF)),
        v((HALF, FB)), v((FB, HALF)),
        v((4, 2, BOTH, FB), F32), v((4, 2, BOTH, FB)), v((4, 2, BOTH, FB)),
        v((FB, 4 * BOTH)), v((FB, 4 * BOTH)), v((4, BOTH, FB)), v((4, BOTH, FB)),
        v((3, 4, BOTH, WW)), v((3, 4, BOTH, WW)), v((3, 4, BOTH, WW), F32),
        v((3, 2, BOTH, 256)), v((3, 2, BOTH, 256)), v((3, 2, BOTH, WW)), v((3, 2, BOTH, WW)),
        v((3, 2, 4, 2, 16, 384)), v((3, 2, 2, 4, 16, 384)),
        v((16, D), F32), v((16, D), F32), v((16, 128), F32),
        v((2, FB, QW)), v((2, FB, QW)), v((2, 2, FB, QW)), v((2, 2, FB, QW)),
        v((2, FB, QW), F32),
        v((4, 8, WW), F32), v((2, 8, 8, WW), F32), v((4, 2, 8, WW), F32),
        pltpu.SemaphoreType.DMA((N_COPIES,)), pltpu.SemaphoreType.DMA((N_COPIES,)),
        pltpu.SemaphoreType.DMA((4,)),
    ]
    return pl.pallas_call(
        body,
        out_shape=(
            jax.ShapeDtypeStruct((16, D), BF16),
            jax.ShapeDtypeStruct((TOK, 16), BF16),
            jax.ShapeDtypeStruct((1, D), F32),
            jax.ShapeDtypeStruct((QW, FB), BF16),
            jax.ShapeDtypeStruct((FB, QW), BF16),
        ),
        in_specs=[vmem, vmem, hbm, hbm, hbm, hbm],
        out_specs=(vmem,) * 5,
        scratch_shapes=scratch,
        compiler_params=pltpu.CompilerParams(
            collective_id=0, has_side_effects=True, vmem_limit_bytes=60 * 2**20
        ),
    )(keep, gain, tokens, cotangent, w_up, w_down)


def merge_body(sel_ref, rows_ref, cot_ref, out_ref):
    sel = sel_ref[...]
    placed = dot(sel, rows_ref[...])
    kept = jnp.sum(sel.astype(F32), axis=1, keepdims=True) > 0.5
    out_ref[...] = jnp.where(kept, placed, cot_ref[...].astype(F32)).astype(BF16)


def merge(sel, rows, cotangent):
    h = 64
    return pl.pallas_call(
        merge_body,
        grid=(TOK // h,),
        out_shape=jax.ShapeDtypeStruct((TOK, D), BF16),
        in_specs=[
            pl.BlockSpec((h, 16), lambda i: (i, 0)),
            pl.BlockSpec((16, D), lambda i: (0, 0)),
            pl.BlockSpec((h, D), lambda i: (i, 0)),
        ],
        out_specs=pl.BlockSpec((h, D), lambda i: (i, 0)),
    )(sel, rows, cotangent)


def local(tokens, gain, w_up, w_down, cotangent, keep_index):
    rows, sel, gain_grad, up, down = kernel_call(
        keep_index, tokens, cotangent, gain.reshape(1, D), w_up, w_down
    )
    return (merge(sel, rows, cotangent), gain_grad.reshape(D), up, down)


def solution(mesh):
    in_specs = (
        P(("replica", "node"), None),
        P(),
        P("replica", "node"),
        P("node", "replica"),
        P(("replica", "node"), None),
        P("replica", None),
    )
    out_specs = (P(("replica", "node"), None), P(), P("replica", "node"), P("node", "replica"))
    return jax.shard_map(local, mesh=mesh, in_specs=in_specs, out_specs=out_specs, check_vma=False)
```

time: 142 us -> 128 us (0.901); the launches traced: 140 us -> 128 us
  Pallas kernels: 131 us -> 125 us
  matrix products: 3.68 us -> 0 us
  local copies, waits for them, and re-layouts: 3.76 us -> 2.25 us
    pallas_call x1, Pallas kernels: 131 us -> 120 us  [kernel_call(): pl.pallas_call(body, out_shape=(jax.ShapeDtypeStruct((16, D), BF16), jax....]
    pallas_call x0 -> x1, Pallas kernels: none -> 4.95 us  [merge(): pl.pallas_call(merge_body, grid=(TOK // h,), out_shape=jax.ShapeDtypeStru...]
    dot_general x1 -> x0, matrix products: 3.68 us -> none  [dot(): lax.dot_general(a, b, (((ca,), (cb,)), ((), ())), preferred_element_type=...]
    unnamed x8 -> x9, local copies, waits for them, and re-layouts: 2.94 us -> 2.25 us
where the time goes in v2:
time: 128 us
  Pallas kernels  125 us (98%)
  local copies, waits for them, and re-layouts  2.25 us (2%)
    pallas_call x1, Pallas kernels, kernel_call(): pl.pallas_call(body, out_shape=(jax.ShapeDtypeStruct((16, D), BF16), jax....  120 us
    pallas_call x1, Pallas kernels, merge(): pl.pallas_call(merge_body, grid=(TOK // h,), out_shape=jax.ShapeDtypeStru...  4.95 us

profile of v2, /device:TPU:1, one launch (start us, length us, event | category | flops | bytes accessed | tf_op | source)
XLA Modules:
  0.0 127.9 jit_solution(14402477971333595574)
XLA Ops:
  0.6 120.0 %shard_map.93 = (bf16[16,6144]{1,0:T(8,128)(2,1)}, bf16[256,16]{1,0:T(8,128)(2,1)}, f32[1,6144]{1,0:T(1,128)}, bf16[768,384]{1,0:T(8,128)(2,1)}, bf16[384,768]{1,0:T(8,128)(2,1)}) custom-call(s32[4,72]{1,0:T(4,128)} %keep_ref.1, f32[1,6144]{1,0:T(1,128)} %bitcast.2, bf16[256,6144]{1,0:T(8,128)(2,1)} %tok_hbm.1, bf16[256,6144]{1,0:T(8,128)(2,1)} %cot_ref.1, ...), custom_call_target="tpu_custom_call" | custom-call | tf_op jit(solution)/shard_map/pallas_call | solution.py:542
  120.7 0.0 copy-start.2
  120.7 0.0 copy-start.1
  120.7 0.0 copy-start
  120.7 4.9 %shard_map.94 = bf16[256,6144]{1,0:T(8,128)(2,1)} custom-call(bf16[256,16]{1,0:T(8,128)(2,1)} %get-tuple-element.9.sel_ref, bf16[16,6144]{1,0:T(8,128)(2,1)} %get-tuple-element.10.rows_ref, bf16[256,6144]{1,0:T(8,128)(2,1)} %cot_ref.1), custom_call_target="tpu_custom_call" | custom-call | tf_op jit(solution)/shard_map/pallas_call | solution.py:569
  125.6 0.0 copy-done.2
  125.6 0.6 copy.13
  126.3 0.0 copy-done.1
  126.3 0.8 copy.14
  127.1 0.0 copy-done
  127.1 0.8 copy.15
Async XLA Ops:
  120.7 5.0 %copy-start.2 = (f32[1,6144]{1,0:T(1,128)S(1)}, f32[1,6144]{1,0:T(1,128)}, u32[]{:S(2)}) copy-start(f32[1,6144]{1,0:T(1,128)} %get-tuple-element.11) | copy-start | bytes 73732
  120.7 5.6 %copy-start.1 = (bf16[768,384]{1,0:T(8,128)(2,1)S(1)}, bf16[768,384]{1,0:T(8,128)(2,1)}, u32[]{:S(2)}) copy-start(bf16[768,384]{1,0:T(8,128)(2,1)} %get-tuple-element.20) | copy-start | bytes 1769476
  120.7 6.4 %copy-start = (bf16[384,768]{1,0:T(8,128)(2,1)S(1)}, bf16[384,768]{1,0:T(8,128)(2,1)}, u32[]{:S(2)}) copy-start(bf16[384,768]{1,0:T(8,128)(2,1)} %get-tuple-element.21) | copy-start | bytes 1769476

commit v3 on v2

--- a/solution.py
+++ b/solution.py
@@ -155,12 +155,20 @@
     nhat_s[...] = nhat
     rstd_s[...] = jnp.broadcast_to(rstd, (16, 128))
     pack(nhat * gain_ref[...], 0)
+    pl.semaphore_wait(barrier, len(peers))
+
+    wu_in.wait()
+    wd_in.wait()
+    wu_r = send(wu_own, wu_own, dev(y_=step(y, 1)))
+    wd_l = send(wd_own, wd_own, dev(y_=step(y, -1)))
+    wu_l = send(wu_own, wu_own, dev(y_=step(y, -1)))
+    wd_r = send(wd_own, wd_own, dev(y_=step(y, 1)))
+
     cot_in.wait()
     dyr = dot(sel, cot_ref[...])
     dy_s[...] = dyr
     pack(dyr, 1)
 
-    pl.semaphore_wait(barrier, len(peers))
 
     first = []
     for k in range(CHUNKS):
@@ -171,13 +179,6 @@
                 send(pks[k].at[c2, zl2], gs[k].at[zl, zh, c], dev(zl_=zl2, c_=c2))
             )
         first.append(group)
-
-    wu_in.wait()
-    wd_in.wait()
-    wu_r = send(wu_own, wu_own, dev(y_=step(y, 1)))
-    wd_l = send(wd_own, wd_own, dev(y_=step(y, -1)))
-    wu_l = send(wu_own, wu_own, dev(y_=step(y, -1)))
-    wd_r = send(wd_own, wd_own, dev(y_=step(y, 1)))
 
     for k in range(CHUNKS):
         gs[k][pl.ds(zl, 1), pl.ds(zh, 1), pl.ds(c, 1)] = pks[k][pl.ds(c, 1), pl.ds(zl, 1)][None]
@@ -255,6 +256,48 @@
             to_sib(-1, s_m, k // 2)
             to_sib(1, s_p, k // 2)
 
+    zp = dev(zl_=1 - zl)
+
+    def forward_part(i, s):
+        if i < 3:
+            pre = dot(t_buf[0, s], wu[...])
+            dac = dot(t_buf[1, s], wd[...], 1, 1)
+        else:
+            pre = jnp.zeros((BOTH, FB), F32)
+            dac = jnp.zeros((BOTH, FB), F32)
+            for k in range(3):
+                sibs[2, k].wait_recv()
+                at = slice(2 * CW * k, 2 * CW * (k + 1))
+                pre = pre + dot(t_buf[0, s, :, at], wu[at])
+                dac = dac + dot(t_buf[1, s, :, at], wd[:, at], 1, 1)
+        keepf[i, 0] = pre
+        keepf[i, 1] = dac
+        psend[i, 0] = pre.astype(BF16)
+        psend[i, 1] = dac.astype(BF16)
+        parts[i] = send(psend.at[i], precv.at[i], zp)
+
+    def middle(i, s):
+        parts[i].wait_recv()
+        v = keepf[i, 0] + precv[i, 0].astype(F32)
+        da = keepf[i, 1] + precv[i, 1].astype(F32)
+        v2 = v * v
+        t = jnp.tanh(A_TANH * (v + B_TANH * v * v2))
+        act = 0.5 * v * (1.0 + t)
+        slope = 0.5 * (1.0 + t) + 0.5 * v * (1.0 - t * t) * (A_TANH * (1.0 + 3.0 * B_TANH * v2))
+        act_b[s] = act.astype(BF16)
+        dpre_b[s] = (da * slope).astype(BF16)
+
+    parts = {}
+
+    def from_sib(i):
+        for k in range(3):
+            sibs[i, k].wait_recv()
+
+    def far_pair(k):
+        fx[2 * k].wait_recv()
+        fx[2 * k + 1].wait_recv()
+        to_sib(2, s_2, k)
+
     z_own(0)
     z_own(1)
     z_next(0)
@@ -271,11 +314,6 @@
     z_next(4)
     pass_on(0)
     order(3)
-    z_next(5)
-    pass_on(1)
-    order(4)
-    pass_on(2)
-    order(5)
 
     def wu_at(y_):
         return wu.at[pl.ds(pl.multiple_of(y_ * QW, QW), QW)]
@@ -287,47 +325,18 @@
     p = col_of(wd, step(y, 1) * QW, QW)
     wd_f = send(p, p, dev(y_=step(y, -1)))
 
-    for k in range(3, CHUNKS):
-        pass_on(k)
-
+    z_next(5)
+    pass_on(1)
+    order(4)
+    pass_on(2)
+    order(5)
+    pass_on(3)
     for d in (wu_l, wd_r, wu_f, wd_f):
         d.wait_recv()
-
-    zp = dev(zl_=1 - zl)
-
-    def forward_part(i, s):
-        pre = dot(t_buf[0, s], wu[...])
-        dac = dot(t_buf[1, s], wd[...], 1, 1)
-        keepf[i, 0] = pre
-        keepf[i, 1] = dac
-        psend[i, 0] = pre.astype(BF16)
-        psend[i, 1] = dac.astype(BF16)
-        parts[i] = send(psend.at[i], precv.at[i], zp)
-
-    def middle(i, s):
-        parts[i].wait_recv()
-        v = keepf[i, 0] + precv[i, 0].astype(F32)
-        da = keepf[i, 1] + precv[i, 1].astype(F32)
-        v2 = v * v
-        t = jnp.tanh(A_TANH * (v + B_TANH * v * v2))
-        act = 0.5 * v * (1.0 + t)
-        slope = 0.5 * (1.0 + t) + 0.5 * v * (1.0 - t * t) * (A_TANH * (1.0 + 3.0 * B_TANH * v2))
-        act_b[s] = act.astype(BF16)
-        dpre_b[s] = (da * slope).astype(BF16)
-
-    parts = {}
-
-    def from_sib(i):
-        for k in range(3):
-            sibs[i, k].wait_recv()
-
-    def far_pair(k):
-        fx[2 * k].wait_recv()
-        fx[2 * k + 1].wait_recv()
-        to_sib(2, s_2, k)
-
     from_sib(0)
     forward_part(0, x)
+    pass_on(4)
+    pass_on(5)
     far_pair(0)
     from_sib(-1)
     forward_part(1, s_m)
@@ -337,7 +346,6 @@
     middle(0, x)
     far_pair(2)
     middle(1, s_m)
-    from_sib(2)
     forward_part(3, s_2)
     middle(2, s_p)
     middle(3, s_2)
@@ -557,33 +565,44 @@
     )(keep, gain, tokens, cotangent, w_up, w_down)
 
 
-def merge_body(sel_ref, rows_ref, cot_ref, out_ref):
+def merge_body(sel_ref, rows_ref, cot_ref, up_ref, down_ref, gain_ref, out_ref, up_out, down_out, gain_out):
     sel = sel_ref[...]
     placed = dot(sel, rows_ref[...])
     kept = jnp.sum(sel.astype(F32), axis=1, keepdims=True) > 0.5
     out_ref[...] = jnp.where(kept, placed, cot_ref[...].astype(F32)).astype(BF16)
-
-
-def merge(sel, rows, cotangent):
-    h = 64
+    up_out[...] = up_ref[...]
+    down_out[...] = down_ref[...]
+    gain_out[...] = gain_ref[...]
+
+
+def merge(sel, rows, cotangent, up, down, gain):
+    steps = 8
+    h = TOK // steps
+
+    def block(*shape):
+        return pl.BlockSpec(shape, lambda i: (i, 0))
+
+    results = [block(h, D), block(QW // steps, FB), block(FB // steps, QW), pl.BlockSpec((1, D), lambda i: (0, 0))]
     return pl.pallas_call(
         merge_body,
-        grid=(TOK // h,),
-        out_shape=jax.ShapeDtypeStruct((TOK, D), BF16),
-        in_specs=[
-            pl.BlockSpec((h, 16), lambda i: (i, 0)),
-            pl.BlockSpec((16, D), lambda i: (0, 0)),
-            pl.BlockSpec((h, D), lambda i: (i, 0)),
-        ],
-        out_specs=pl.BlockSpec((h, D), lambda i: (i, 0)),
-    )(sel, rows, cotangent)
+        grid=(steps,),
+        out_shape=(
+            jax.ShapeDtypeStruct((TOK, D), BF16),
+            jax.ShapeDtypeStruct((QW, FB), BF16),
+            jax.ShapeDtypeStruct((FB, QW), BF16),
+            jax.ShapeDtypeStruct((1, D), F32),
+        ),
+        in_specs=[block(h, 16), pl.BlockSpec((16, D), lambda i: (0, 0))] + results,
+        out_specs=results,
+    )(sel, rows, cotangent, up, down, gain)
 
 
 def local(tokens, gain, w_up, w_down, cotangent, keep_index):
     rows, sel, gain_grad, up, down = kernel_call(
         keep_index, tokens, cotangent, gain.reshape(1, D), w_up, w_down
     )
-    return (merge(sel, rows, cotangent), gain_grad.reshape(D), up, down)
+    input_grad, up, down, gain_grad = merge(sel, rows, cotangent, up, down, gain_grad)
+    return (input_grad, gain_grad.reshape(D), up, down)
 
 
 def solution(mesh):

time: 128 us -> 128 us (level)
  local copies, waits for them, and re-layouts: 2.25 us -> 0 us
  Pallas kernels: 125 us -> 127 us
    pallas_call x1, Pallas kernels: 4.95 us -> 7.44 us  [merge(): pl.pallas_call(merge_body, grid=(steps,), out_shape=(jax.ShapeDtypeStruct...]
    unnamed x9 -> x0, local copies, waits for them, and re-layouts: 2.25 us -> none
where the time goes in v3:
time: 128 us
  Pallas kernels  127 us (99%)
    pallas_call x1, Pallas kernels, kernel_call(): pl.pallas_call(body, out_shape=(jax.ShapeDtypeStruct((16, D), BF16), jax....  120 us
    pallas_call x1, Pallas kernels, merge(): pl.pallas_call(merge_body, grid=(steps,), out_shape=(jax.ShapeDtypeStruct...  7.44 us

profile of v3, /device:TPU:1, one launch (start us, length us, event | category | flops | bytes accessed | tf_op | source)
XLA Modules:
  0.0 127.8 jit_solution(7899334929307214721)
XLA Ops:
  0.6 119.6 %shard_map.93 = (bf16[16,6144]{1,0:T(8,128)(2,1)}, bf16[256,16]{1,0:T(8,128)(2,1)}, f32[1,6144]{1,0:T(1,128)}, bf16[768,384]{1,0:T(8,128)(2,1)}, bf16[384,768]{1,0:T(8,128)(2,1)}) custom-call(s32[4,72]{1,0:T(4,128)} %keep_ref.1, f32[1,6144]{1,0:T(1,128)} %bitcast.2, bf16[256,6144]{1,0:T(8,128)(2,1)} %tok_hbm.1, bf16[256,6144]{1,0:T(8,128)(2,1)} %cot_ref.1, ...), custom_call_target="tpu_custom_call" | custom-call | tf_op jit(solution)/shard_map/pallas_call | solution.py:550
  120.2 7.4 %shard_map.94 = (bf16[256,6144]{1,0:T(8,128)(2,1)}, bf16[768,384]{1,0:T(8,128)(2,1)}, bf16[384,768]{1,0:T(8,128)(2,1)}, f32[1,6144]{1,0:T(1,128)}) custom-call(bf16[256,16]{1,0:T(8,128)(2,1)} %get-tuple-element.13.sel_ref, bf16[16,6144]{1,0:T(8,128)(2,1)} %get-tuple-element.14.rows_ref, bf16[256,6144]{1,0:T(8,128)(2,1)} %cot_ref.1, ...), custom_call_target="tpu_custom_call" | custom-call | tf_op jit(solution)/shard_map/pallas_call | solution.py:586

commit v4 on v3

--- a/solution.py
+++ b/solution.py
@@ -94,12 +94,15 @@
     peers += [dev(y_=step(y, d)) for d in (1, 2, 3)]
     for p in peers:
         pl.semaphore_signal(barrier, inc=1, device_id=p, device_id_type=MESH)
-    tok_in = fetch(tok_hbm, tok_ref, 0)
-    cot_in = fetch(cot_hbm, cot_ref, 1)
+    tok_in, cot_in = [], []
+    for ref, to, ins, k in ((tok_hbm, tok_ref, tok_in, 2), (cot_hbm, cot_ref, cot_in, 6)):
+        for i in range(4):
+            at = pl.ds(64 * i, 64)
+            ins.append(fetch(ref.at[at], to.at[at], k + i))
     wu_own = wu.at[pl.ds(pl.multiple_of(y * QW, QW), QW)]
     wd_own = col_of(wd, y * QW, QW)
-    wu_in = fetch(wup_ref, wu_own, 2)
-    wd_in = fetch(wdn_ref, wd_own, 3)
+    wu_in = fetch(wup_ref, wu_own, 0)
+    wd_in = fetch(wdn_ref, wd_own, 1)
 
     n8 = lax.rem(n, 8)
     kv = keep_ref[pl.ds(x, 1), :]
@@ -146,7 +149,8 @@
                 pks[k][a, h, :, 256:384] = extra.astype(BF16)
             pk0[a, h, :, 384:512] = meta
 
-    tok_in.wait()
+    for d in tok_in:
+        d.wait()
     xr = dot(sel, tok_ref[...])
     mean = jnp.mean(xr, axis=1, keepdims=True)
     cen = xr - mean
@@ -164,7 +168,8 @@
     wu_l = send(wu_own, wu_own, dev(y_=step(y, -1)))
     wd_r = send(wd_own, wd_own, dev(y_=step(y, 1)))
 
-    cot_in.wait()
+    for d in cot_in:
+        d.wait()
     dyr = dot(sel, cot_ref[...])
     dy_s[...] = dyr
     pack(dyr, 1)
@@ -312,7 +317,6 @@
     order(2)
     z_own(5)
     z_next(4)
-    pass_on(0)
     order(3)
 
     def wu_at(y_):
@@ -326,32 +330,28 @@
     wd_f = send(p, p, dev(y_=step(y, -1)))
 
     z_next(5)
-    pass_on(1)
     order(4)
-    pass_on(2)
     order(5)
-    pass_on(3)
+    for k in range(CHUNKS):
+        pass_on(k)
     for d in (wu_l, wd_r, wu_f, wd_f):
         d.wait_recv()
     from_sib(0)
     forward_part(0, x)
-    pass_on(4)
-    pass_on(5)
-    far_pair(0)
     from_sib(-1)
     forward_part(1, s_m)
-    far_pair(1)
     from_sib(1)
     forward_part(2, s_p)
+    far_pair(0)
     middle(0, x)
+    far_pair(1)
+    middle(1, s_m)
     far_pair(2)
-    middle(1, s_m)
     forward_part(3, s_2)
     middle(2, s_p)
     middle(3, s_2)
 
     dpre_t[...] = dpre_b[...].reshape(4 * BOTH, FB).astype(F32).T.astype(BF16)
-    act_t[...] = act_b[...].reshape(4 * BOTH, FB).astype(F32).T.astype(BF16)
 
     def rows_of(a, q):
         v = t_buf[a, :, :, pl.ds(pl.multiple_of(q * QW, 128), QW)]
@@ -367,6 +367,7 @@
     q_p, q_m, q_2 = step(y, 1), step(y, -1), step(y, 2)
     ys1[0] = up_part(q_2).astype(BF16)
     y1u = send(ys1.at[0], yr1.at[0], yp)
+    act_t[...] = act_b[...].reshape(4 * BOTH, FB).astype(F32).T.astype(BF16)
     ys1[1] = down_part(q_2).astype(BF16)
     y1d = send(ys1.at[1], yr1.at[1], ym)
 
@@ -545,7 +546,7 @@
         v((2, FB, QW), F32),
         v((4, 8, WW), F32), v((2, 8, 8, WW), F32), v((4, 2, 8, WW), F32),
         pltpu.SemaphoreType.DMA((N_COPIES,)), pltpu.SemaphoreType.DMA((N_COPIES,)),
-        pltpu.SemaphoreType.DMA((4,)),
+        pltpu.SemaphoreType.DMA((10,)),
     ]
     return pl.pallas_call(
         body,
@@ -565,35 +566,57 @@
     )(keep, gain, tokens, cotangent, w_up, w_down)
 
 
-def merge_body(sel_ref, rows_ref, cot_ref, up_ref, down_ref, gain_ref, out_ref, up_out, down_out, gain_out):
-    sel = sel_ref[...]
-    placed = dot(sel, rows_ref[...])
-    kept = jnp.sum(sel.astype(F32), axis=1, keepdims=True) > 0.5
-    out_ref[...] = jnp.where(kept, placed, cot_ref[...].astype(F32)).astype(BF16)
-    up_out[...] = up_ref[...]
-    down_out[...] = down_ref[...]
-    gain_out[...] = gain_ref[...]
+STEPS = 8
+
+
+def merge_body(
+    sel_ref, rows_ref, cot_ref, up_ref, down_ref, gain_ref,
+    out_ref, up_out, down_out, gain_out, buf, isem, osem, rsem,
+):
+    h = TOK // STEPS
+    ins = []
+    for i in range(STEPS):
+        at = pl.ds(h * i, h)
+        ins.append(pltpu.make_async_copy(cot_ref.at[at], buf.at[at], isem.at[i]))
+        ins[-1].start()
+    waits = []
+    for i, (a, b) in enumerate(((up_ref, up_out), (down_ref, down_out), (gain_ref, gain_out))):
+        waits.append(pltpu.make_async_copy(a, b, rsem.at[i]))
+        waits[-1].start()
+    rows = rows_ref[...]
+    for i in range(STEPS):
+        at = slice(h * i, h * (i + 1))
+        sel = sel_ref[at, :]
+        kept = jnp.sum(sel.astype(F32), axis=1, keepdims=True) > 0.5
+        placed = dot(sel, rows)
+        ins[i].wait()
+        buf[at, :] = jnp.where(kept, placed, buf[at, :].astype(F32)).astype(BF16)
+        at = pl.ds(h * i, h)
+        waits.append(pltpu.make_async_copy(buf.at[at], out_ref.at[at], osem.at[i]))
+        waits[-1].start()
+    for d in waits:
+        d.wait()
 
 
 def merge(sel, rows, cotangent, up, down, gain):
-    steps = 8
-    h = TOK // steps
-
-    def block(*shape):
-        return pl.BlockSpec(shape, lambda i: (i, 0))
-
-    results = [block(h, D), block(QW // steps, FB), block(FB // steps, QW), pl.BlockSpec((1, D), lambda i: (0, 0))]
+    vmem = pl.BlockSpec(memory_space=pltpu.VMEM)
+    hbm = pl.BlockSpec(memory_space=pl.ANY)
     return pl.pallas_call(
         merge_body,
-        grid=(steps,),
         out_shape=(
             jax.ShapeDtypeStruct((TOK, D), BF16),
             jax.ShapeDtypeStruct((QW, FB), BF16),
             jax.ShapeDtypeStruct((FB, QW), BF16),
             jax.ShapeDtypeStruct((1, D), F32),
         ),
-        in_specs=[block(h, 16), pl.BlockSpec((16, D), lambda i: (0, 0))] + results,
-        out_specs=results,
+        in_specs=[vmem, vmem, hbm, hbm, hbm, hbm],
+        out_specs=(hbm,) * 4,
+        scratch_shapes=[
+            pltpu.VMEM((TOK, D), BF16),
+            pltpu.SemaphoreType.DMA((STEPS,)),
+            pltpu.SemaphoreType.DMA((STEPS,)),
+            pltpu.SemaphoreType.DMA((3,)),
+        ],
     )(sel, rows, cotangent, up, down, gain)
 
 

time: 128 us -> 160 us (1.25)
  Pallas kernels: 127 us -> 159 us
    pallas_call x1, Pallas kernels: 7.44 us -> 38.7 us  [merge(): pl.pallas_call(merge_body, out_shape=(jax.ShapeDtypeStruct((TOK, D), BF16...]
where the time goes in v4:
time: 160 us
  Pallas kernels  159 us (99%)
    pallas_call x1, Pallas kernels, kernel_call(): pl.pallas_call(body, out_shape=(jax.ShapeDtypeStruct((16, D), BF16), jax....  120 us
    pallas_call x1, Pallas kernels, merge(): pl.pallas_call(merge_body, out_shape=(jax.ShapeDtypeStruct((TOK, D), BF16...  38.7 us

profile of v4, /device:TPU:1, one launch (start us, length us, event | category | flops | bytes accessed | tf_op | source)
XLA Modules:
  0.0 160.0 jit_solution(4848785757245840178)
XLA Ops:
  0.6 120.4 %shard_map.93 = (bf16[16,6144]{1,0:T(8,128)(2,1)}, bf16[256,16]{1,0:T(8,128)(2,1)}, f32[1,6144]{1,0:T(1,128)}, bf16[768,384]{1,0:T(8,128)(2,1)}, bf16[384,768]{1,0:T(8,128)(2,1)}) custom-call(s32[4,72]{1,0:T(4,128)} %keep_ref.1, f32[1,6144]{1,0:T(1,128)} %bitcast.2, bf16[256,6144]{1,0:T(8,128)(2,1)} %tok_hbm.1, bf16[256,6144]{1,0:T(8,128)(2,1)} %cot_ref.1, ...), custom_call_target="tpu_custom_call" | custom-call | tf_op jit(solution)/shard_map/pallas_call | solution.py:551
  121.1 38.7 %shard_map.94 = (bf16[256,6144]{1,0:T(8,128)(2,1)}, bf16[768,384]{1,0:T(8,128)(2,1)}, bf16[384,768]{1,0:T(8,128)(2,1)}, f32[1,6144]{1,0:T(1,128)}) custom-call(bf16[256,16]{1,0:T(8,128)(2,1)} %get-tuple-element.13.sel_ref, bf16[16,6144]{1,0:T(8,128)(2,1)} %get-tuple-element.14.rows_ref, bf16[256,6144]{1,0:T(8,128)(2,1)} %cot_ref.1, ...), custom_call_target="tpu_custom_call" | custom-call | tf_op jit(solution)/shard_map/pallas_call | solution.py:604

commit v5 on v4

--- a/solution.py
+++ b/solution.py
@@ -38,7 +38,7 @@
 
 def body(
     keep_ref, gain_ref, tok_hbm, cot_hbm, wup_ref, wdn_ref,
-    rows_ref, sel_ref, gout_ref, upg_ref, dng_ref,
+    rows_ref, sel_ref, kept_ref, gout_ref, upg_ref, dng_ref,
     tok_ref, cot_ref, pk0, pkn, g0, gn, ordered, t_buf, wu, wd,
     keepf, psend, precv, act_t, dpre_t, act_b, dpre_b,
     csend, crecv, cown, xs1, xr1, xs2, xr2, zs, zr, nhat_s, dy_s, rstd_s,
@@ -116,7 +116,9 @@
     pos = jnp.sum(jnp.where(hit, local_pos, 0.0), axis=1, keepdims=True)
     live = iota((16, TOK), 0).astype(F32) < mine
     sel = jnp.where((iota((16, TOK), 1).astype(F32) == pos) & live, 1.0, 0.0).astype(BF16)
-    sel_ref[...] = sel.astype(F32).T.astype(BF16)
+    sel_t = sel.astype(F32).T
+    sel_ref[...] = sel_t.astype(BF16)
+    kept_ref[...] = jnp.sum(sel_t, axis=1, keepdims=True)
 
     row_i, lane_i = iota((16, 128), 0), iota((16, 128), 1)
     kind = lax.rem(row_i, 8)
@@ -149,6 +151,32 @@
                 pks[k][a, h, :, 256:384] = extra.astype(BF16)
             pk0[a, h, :, 384:512] = meta
 
+    pl.semaphore_wait(barrier, len(peers))
+
+    y_p, y_m = dev(y_=step(y, 1)), dev(y_=step(y, -1))
+    wu_in.wait()
+    wu_r, wu_l = send(wu_own, wu_own, y_p), send(wu_own, wu_own, y_m)
+    wd_in.wait()
+
+    def pass_w_up():
+        wu_r.wait_recv()
+        p = wu.at[pl.ds(pl.multiple_of(step(y, -1) * QW, QW), QW // 2)]
+        a = send(p, p, y_p)
+        wu_l.wait_recv()
+        p = wu.at[pl.ds(pl.multiple_of(step(y, 1) * QW + QW // 2, QW // 2), QW // 2)]
+        return a, send(p, p, y_m)
+
+    def send_w_down():
+        return send(wd_own, wd_own, y_p), send(wd_own, wd_own, y_m)
+
+    def pass_w_down(own):
+        own[0].wait_recv()
+        p = col_of(wd, step(y, -1) * QW, QW // 2)
+        a = send(p, p, y_p)
+        own[1].wait_recv()
+        p = col_of(wd, step(y, 1) * QW + QW // 2, QW // 2)
+        return a, send(p, p, y_m)
+
     for d in tok_in:
         d.wait()
     xr = dot(sel, tok_ref[...])
@@ -159,15 +187,6 @@
     nhat_s[...] = nhat
     rstd_s[...] = jnp.broadcast_to(rstd, (16, 128))
     pack(nhat * gain_ref[...], 0)
-    pl.semaphore_wait(barrier, len(peers))
-
-    wu_in.wait()
-    wd_in.wait()
-    wu_r = send(wu_own, wu_own, dev(y_=step(y, 1)))
-    wd_l = send(wd_own, wd_own, dev(y_=step(y, -1)))
-    wu_l = send(wu_own, wu_own, dev(y_=step(y, -1)))
-    wd_r = send(wd_own, wd_own, dev(y_=step(y, 1)))
-
     for d in cot_in:
         d.wait()
     dyr = dot(sel, cot_ref[...])
@@ -263,26 +282,32 @@
 
     zp = dev(zl_=1 - zl)
 
-    def forward_part(i, s):
-        if i < 3:
-            pre = dot(t_buf[0, s], wu[...])
-            dac = dot(t_buf[1, s], wd[...], 1, 1)
-        else:
-            pre = jnp.zeros((BOTH, FB), F32)
-            dac = jnp.zeros((BOTH, FB), F32)
-            for k in range(3):
-                sibs[2, k].wait_recv()
-                at = slice(2 * CW * k, 2 * CW * (k + 1))
-                pre = pre + dot(t_buf[0, s, :, at], wu[at])
-                dac = dac + dot(t_buf[1, s, :, at], wd[:, at], 1, 1)
-        keepf[i, 0] = pre
-        keepf[i, 1] = dac
-        psend[i, 0] = pre.astype(BF16)
-        psend[i, 1] = dac.astype(BF16)
-        parts[i] = send(psend.at[i], precv.at[i], zp)
+    def give(i, j, v):
+        keepf[i, j] = v
+        psend[i, j] = v.astype(BF16)
+        parts[i, j] = send(psend.at[i, j], precv.at[i, j], zp)
+
+    def pre_part(i, s):
+        give(i, 0, dot(t_buf[0, s], wu[...]))
+
+    def dac_part(i, s):
+        give(i, 1, dot(t_buf[1, s], wd[...], 1, 1))
+
+    def far_parts():
+        pre = jnp.zeros((BOTH, FB), F32)
+        dac = jnp.zeros((BOTH, FB), F32)
+        for k in range(3):
+            sibs[2, k].wait_recv()
+            at = slice(2 * CW * k, 2 * CW * (k + 1))
+            pre = pre + dot(t_buf[0, s_2, :, at], wu[at])
+            if k == 2:
+                give(3, 0, pre)
+            dac = dac + dot(t_buf[1, s_2, :, at], wd[:, at], 1, 1)
+        give(3, 1, dac)
 
     def middle(i, s):
-        parts[i].wait_recv()
+        parts[i, 0].wait_recv()
+        parts[i, 1].wait_recv()
         v = keepf[i, 0] + precv[i, 0].astype(F32)
         da = keepf[i, 1] + precv[i, 1].astype(F32)
         v2 = v * v
@@ -308,6 +333,8 @@
     z_next(0)
     z_own(2)
     z_next(1)
+    wu_far = pass_w_up()
+    wd_near = send_w_down()
     order(0)
     z_own(3)
     z_next(2)
@@ -319,35 +346,35 @@
     z_next(4)
     order(3)
 
-    def wu_at(y_):
-        return wu.at[pl.ds(pl.multiple_of(y_ * QW, QW), QW)]
-
-    wu_r.wait_recv()
-    p = wu_at(step(y, -1))
-    wu_f = send(p, p, dev(y_=step(y, 1)))
-    wd_l.wait_recv()
-    p = col_of(wd, step(y, 1) * QW, QW)
-    wd_f = send(p, p, dev(y_=step(y, -1)))
-
     z_next(5)
     order(4)
     order(5)
-    for k in range(CHUNKS):
-        pass_on(k)
-    for d in (wu_l, wd_r, wu_f, wd_f):
+    pass_on(0)
+    pass_on(1)
+    for d in wu_far:
         d.wait_recv()
     from_sib(0)
-    forward_part(0, x)
+    pre_part(0, x)
+    pass_on(2)
+    pass_on(3)
+    wd_far = pass_w_down(wd_near)
+    pass_on(4)
+    pass_on(5)
     from_sib(-1)
-    forward_part(1, s_m)
+    pre_part(1, s_m)
     from_sib(1)
-    forward_part(2, s_p)
+    pre_part(2, s_p)
+    for d in wd_far:
+        d.wait_recv()
+    dac_part(0, x)
+    dac_part(1, s_m)
+    dac_part(2, s_p)
     far_pair(0)
+    far_pair(1)
     middle(0, x)
-    far_pair(1)
+    far_pair(2)
     middle(1, s_m)
-    far_pair(2)
-    forward_part(3, s_2)
+    far_parts()
     middle(2, s_p)
     middle(3, s_2)
 
@@ -363,7 +390,7 @@
     def down_part(q):
         return dot(act_t[...], rows_of(1, q))
 
-    yp, ym = dev(y_=step(y, 1)), dev(y_=step(y, -1))
+    yp, ym = y_p, y_m
     q_p, q_m, q_2 = step(y, 1), step(y, -1), step(y, 2)
     ys1[0] = up_part(q_2).astype(BF16)
     y1u = send(ys1.at[0], yr1.at[0], yp)
@@ -553,12 +580,13 @@
         out_shape=(
             jax.ShapeDtypeStruct((16, D), BF16),
             jax.ShapeDtypeStruct((TOK, 16), BF16),
+            jax.ShapeDtypeStruct((TOK, 1), F32),
             jax.ShapeDtypeStruct((1, D), F32),
             jax.ShapeDtypeStruct((QW, FB), BF16),
             jax.ShapeDtypeStruct((FB, QW), BF16),
         ),
         in_specs=[vmem, vmem, hbm, hbm, hbm, hbm],
-        out_specs=(vmem,) * 5,
+        out_specs=(vmem,) * 6,
         scratch_shapes=scratch,
         compiler_params=pltpu.CompilerParams(
             collective_id=0, has_side_effects=True, vmem_limit_bytes=60 * 2**20
@@ -566,65 +594,11 @@
     )(keep, gain, tokens, cotangent, w_up, w_down)
 
 
-STEPS = 8
-
-
-def merge_body(
-    sel_ref, rows_ref, cot_ref, up_ref, down_ref, gain_ref,
-    out_ref, up_out, down_out, gain_out, buf, isem, osem, rsem,
-):
-    h = TOK // STEPS
-    ins = []
-    for i in range(STEPS):
-        at = pl.ds(h * i, h)
-        ins.append(pltpu.make_async_copy(cot_ref.at[at], buf.at[at], isem.at[i]))
-        ins[-1].start()
-    waits = []
-    for i, (a, b) in enumerate(((up_ref, up_out), (down_ref, down_out), (gain_ref, gain_out))):
-        waits.append(pltpu.make_async_copy(a, b, rsem.at[i]))
-        waits[-1].start()
-    rows = rows_ref[...]
-    for i in range(STEPS):
-        at = slice(h * i, h * (i + 1))
-        sel = sel_ref[at, :]
-        kept = jnp.sum(sel.astype(F32), axis=1, keepdims=True) > 0.5
-        placed = dot(sel, rows)
-        ins[i].wait()
-        buf[at, :] = jnp.where(kept, placed, buf[at, :].astype(F32)).astype(BF16)
-        at = pl.ds(h * i, h)
-        waits.append(pltpu.make_async_copy(buf.at[at], out_ref.at[at], osem.at[i]))
-        waits[-1].start()
-    for d in waits:
-        d.wait()
-
-
-def merge(sel, rows, cotangent, up, down, gain):
-    vmem = pl.BlockSpec(memory_space=pltpu.VMEM)
-    hbm = pl.BlockSpec(memory_space=pl.ANY)
-    return pl.pallas_call(
-        merge_body,
-        out_shape=(
-            jax.ShapeDtypeStruct((TOK, D), BF16),
-            jax.ShapeDtypeStruct((QW, FB), BF16),
-            jax.ShapeDtypeStruct((FB, QW), BF16),
-            jax.ShapeDtypeStruct((1, D), F32),
-        ),
-        in_specs=[vmem, vmem, hbm, hbm, hbm, hbm],
-        out_specs=(hbm,) * 4,
-        scratch_shapes=[
-            pltpu.VMEM((TOK, D), BF16),
-            pltpu.SemaphoreType.DMA((STEPS,)),
-            pltpu.SemaphoreType.DMA((STEPS,)),
-            pltpu.SemaphoreType.DMA((3,)),
-        ],
-    )(sel, rows, cotangent, up, down, gain)
-
-
 def local(tokens, gain, w_up, w_down, cotangent, keep_index):
-    rows, sel, gain_grad, up, down = kernel_call(
+    rows, sel, kept, gain_grad, up, down = kernel_call(
         keep_index, tokens, cotangent, gain.reshape(1, D), w_up, w_down
     )
-    input_grad, up, down, gain_grad = merge(sel, rows, cotangent, up, down, gain_grad)
+    input_grad = jnp.where(kept > 0.5, dot(sel, rows).astype(BF16), cotangent)
     return (input_grad, gain_grad.reshape(D), up, down)
 
 

time: 160 us -> 127 us (0.79)
  Pallas kernels: 159 us -> 119 us
  matrix products: 0 us -> 3.67 us
  local copies, waits for them, and re-layouts: 0 us -> 2.26 us
    pallas_call x1 -> x0, Pallas kernels: 38.7 us -> none  [merge(): pl.pallas_call(merge_body, out_shape=(jax.ShapeDtypeStruct((TOK, D), BF16...]
    dot_general x0 -> x1, matrix products: none -> 3.67 us  [dot(): lax.dot_general(a, b, (((ca,), (cb,)), ((), ())), preferred_element_type=...]
    unnamed x0 -> x11, local copies, waits for them, and re-layouts: none -> 2.26 us
where the time goes in v5:
time: 127 us
  Pallas kernels  119 us (94%)
  matrix products  3.67 us (3%)
  local copies, waits for them, and re-layouts  2.26 us (2%)
    pallas_call x1, Pallas kernels, kernel_call(): pl.pallas_call(body, out_shape=(jax.ShapeDtypeStruct((16, D), BF16), jax....  119 us
    dot_general x1, matrix products, dot(): lax.dot_general(a, b, (((ca,), (cb,)), ((), ())), preferred_element_type=...  3.67 us

profile of v5, /device:TPU:1, one launch (start us, length us, event | category | flops | bytes accessed | tf_op | source)
XLA Modules:
  0.0 127.1 jit_solution(16469617612549100375)
XLA Ops:
  0.6 0.0 copy-start
  0.6 119.5 %shard_map.93 = (bf16[16,6144]{1,0:T(8,128)(2,1)}, bf16[256,16]{1,0:T(8,128)(2,1)}, f32[256,1]{1,0:T(8,128)}, f32[1,6144]{1,0:T(1,128)}, bf16[768,384]{1,0:T(8,128)(2,1)}, /*index=5*/bf16[384,768]{1,0:T(8,128)(2,1)}) custom-call(s32[4,72]{1,0:T(4,128)} %keep_ref.1, f32[1,6144]{1,0:T(1,128)} %bitcast.4, bf16[256,6144]{1,0:T(8,128)(2,1)} %tok_hbm.1, ...), custom_call_target="tpu_custom_call" | custom-call | tf_op jit(solution)/shard_map/pallas_call | solution.py:578
  120.1 1.0 compare_reduce_fusion
  121.2 0.0 copy-done
  121.2 0.0 copy-start.3
  121.2 0.0 copy-start.2
  121.2 0.0 copy-start.1
  121.2 3.7 %fusion = bf16[256,6144]{1,0:T(8,128)(2,1)} fusion(bf16[256,6144]{1,0:T(8,128)(2,1)S(1)} %copy-done, bf16[256,16]{1,0:T(8,128)(2,1)} %get-tuple-element.11, bf16[16,6144]{1,0:T(8,128)(2,1)} %get-tuple-element.12, pred[256]{0:T(512)(128)(4,1)S(1)} %compare_reduce_fusion), kind=kOutput, calls=%fused_computation.1 | convolution fusion | flops 53477376 | bytes 6496512 | tf_op jit(solution)/shard_map/dot_general | solution.py:32
  124.9 0.0 copy-done.3
  124.9 0.6 copy.13
  125.5 0.0 copy-done.2
  125.5 0.8 copy.14
  126.3 0.0 copy-done.1
  126.3 0.8 copy.15
Async XLA Ops:
  0.6 120.5 %copy-start = (bf16[256,6144]{1,0:T(8,128)(2,1)S(1)}, bf16[256,6144]{1,0:T(8,128)(2,1)}, u32[]{:S(2)}) copy-start(bf16[256,6144]{1,0:T(8,128)(2,1)} %cot_hbm.1) | copy-start | bytes 9437188
  121.2 3.7 %copy-start.3 = (f32[1,6144]{1,0:T(1,128)S(1)}, f32[1,6144]{1,0:T(1,128)}, u32[]{:S(2)}) copy-start(f32[1,6144]{1,0:T(1,128)} %get-tuple-element.13) | copy-start | bytes 73732
  121.2 4.3 %copy-start.2 = (bf16[768,384]{1,0:T(8,128)(2,1)S(1)}, bf16[768,384]{1,0:T(8,128)(2,1)}, u32[]{:S(2)}) copy-start(bf16[768,384]{1,0:T(8,128)(2,1)} %get-tuple-element.22) | copy-start | bytes 1769476
  121.2 5.1 %copy-start.1 = (bf16[384,768]{1,0:T(8,128)(2,1)S(1)}, bf16[384,768]{1,0:T(8,128)(2,1)}, u32[]{:S(2)}) copy-start(bf16[384,768]{1,0:T(8,128)(2,1)} %get-tuple-element.23) | copy-start | bytes 1769476

commit v6 on v5

--- a/solution.py
+++ b/solution.py
@@ -38,10 +38,10 @@
 
 def body(
     keep_ref, gain_ref, tok_hbm, cot_hbm, wup_ref, wdn_ref,
-    rows_ref, sel_ref, kept_ref, gout_ref, upg_ref, dng_ref,
+    rows_ref, sel_ref, gout_ref, upg_ref, dng_ref,
     tok_ref, cot_ref, pk0, pkn, g0, gn, ordered, t_buf, wu, wd,
     keepf, psend, precv, act_t, dpre_t, act_b, dpre_b,
-    csend, crecv, cown, xs1, xr1, xs2, xr2, zs, zr, nhat_s, dy_s, rstd_s,
+    csend, crecv, cown, xs1, xr1, xs2, xr2, zs, zr, nhat_s, rstd_s,
     ys1, yr1, ys2, yr2, ykeep, gx, gz, gy,
     ssem, rsem, lsem,
 ):
@@ -116,9 +116,8 @@
     pos = jnp.sum(jnp.where(hit, local_pos, 0.0), axis=1, keepdims=True)
     live = iota((16, TOK), 0).astype(F32) < mine
     sel = jnp.where((iota((16, TOK), 1).astype(F32) == pos) & live, 1.0, 0.0).astype(BF16)
-    sel_t = sel.astype(F32).T
-    sel_ref[...] = sel_t.astype(BF16)
-    kept_ref[...] = jnp.sum(sel_t, axis=1, keepdims=True)
+    sel_f = sel.astype(F32)
+    sel_ref[...] = jnp.concatenate([sel_f, sel_f], axis=0).T.astype(BF16)
 
     row_i, lane_i = iota((16, 128), 0), iota((16, 128), 1)
     kind = lax.rem(row_i, 8)
@@ -189,20 +188,8 @@
     pack(nhat * gain_ref[...], 0)
     for d in cot_in:
         d.wait()
-    dyr = dot(sel, cot_ref[...])
-    dy_s[...] = dyr
-    pack(dyr, 1)
-
-
-    first = []
-    for k in range(CHUNKS):
-        group = []
-        for b, e in ((0, 1), (1, 0), (1, 1)):
-            zl2, c2 = lax.rem(zl + b, 2), lax.rem(c + e, 2)
-            group.append(
-                send(pks[k].at[c2, zl2], gs[k].at[zl, zh, c], dev(zl_=zl2, c_=c2))
-            )
-        first.append(group)
+    pack(dot(sel, cot_ref[...]), 1)
+
 
     for k in range(CHUNKS):
         gs[k][pl.ds(zl, 1), pl.ds(zh, 1), pl.ds(c, 1)] = pks[k][pl.ds(c, 1), pl.ds(zl, 1)][None]
@@ -215,17 +202,21 @@
     oh = []
 
     def z_own(k):
-        for d in first[k]:
+        for dz in (1, 3, 0):
+            ring[k, dz] = []
+            for b, e in ((0, 1), (1, 0), (1, 1), (0, 0)):
+                if dz or b or e:
+                    zl2, c2 = lax.rem(zl + b, 2), lax.rem(c + e, 2)
+                    ring[k, dz].append(
+                        send(pks[k].at[c2, zl2], gs[k].at[zl, zh, c], z_peer(dz, b, e))
+                    )
+
+    def z_next(k):
+        for d in ring[k, 1]:
             d.wait_recv()
-        ring[k] = (
-            send(gs[k].at[:, zh], gs[k].at[:, zh], up_z),
-            send(gs[k].at[:, zh], gs[k].at[:, zh], dn_z),
-        )
-
-    def z_next(k):
-        ring[k][0].wait_recv()
         f0 = send(gs[k].at[:, step(zh, -1), 0], gs[k].at[:, step(zh, -1), 0], up_z)
-        ring[k][1].wait_recv()
+        for d in ring[k, 3]:
+            d.wait_recv()
         f1 = send(gs[k].at[:, step(zh, 1), 1], gs[k].at[:, step(zh, 1), 1], dn_z)
         ring2[k] = (f0, f1)
 
@@ -242,6 +233,8 @@
         return t_buf.at[a, s, :, pl.ds(k * CW, CW)]
 
     def order(k):
+        for d in ring[k, 0]:
+            d.wait_recv()
         for d in ring2[k]:
             d.wait_recv()
         if k == 0:
@@ -528,7 +521,10 @@
     h = d_norm * gain_ref[...]
     nh = nhat_s[...]
     inner = h - jnp.mean(h, axis=1, keepdims=True) - nh * jnp.mean(h * nh, axis=1, keepdims=True)
-    rows_ref[...] = (dy_s[...] + rstd_s[:, 0:1] * inner).astype(BF16)
+    d_rows = rstd_s[:, 0:1] * inner
+    high = d_rows.astype(BF16)
+    rows_ref[0:16, :] = high
+    rows_ref[16:32, :] = (d_rows - high.astype(F32)).astype(BF16)
 
     for d in gain3:
         d.wait_recv()
@@ -538,16 +534,20 @@
             at = slice(h * HALF + i * WW, h * HALF + (i + 1) * WW)
             gout_ref[:, at] = g[i:i + 1, :] / gain_ref[:, at]
 
-    for d in (y2pd, y2mu, y2pu, y2md):
-        d.wait_recv()
-    dng_ref[...] = (ykeep[1] + yr2[0, 1].astype(F32) + yr2[1, 1].astype(F32)).astype(BF16)
-    upg_ref[...] = (ykeep[0] + yr2[0, 0].astype(F32) + yr2[1, 0].astype(F32)).T.astype(BF16)
+    y2mu.wait_recv()
+    ykeep[0] += yr2[1, 0].astype(F32)
+    y2pd.wait_recv()
+    ykeep[1] += yr2[0, 1].astype(F32)
+    y2pu.wait_recv()
+    upg_ref[...] = (ykeep[0] + yr2[0, 0].astype(F32)).T.astype(BF16)
+    y2md.wait_recv()
+    dng_ref[...] = (ykeep[1] + yr2[1, 1].astype(F32)).astype(BF16)
 
     for d in started:
         d.wait_send()
 
 
-N_COPIES = 192
+N_COPIES = 256
 
 
 def kernel_call(keep, tokens, cotangent, gain, w_up, w_down):
@@ -568,7 +568,7 @@
         v((3, 4, BOTH, WW)), v((3, 4, BOTH, WW)), v((3, 4, BOTH, WW), F32),
         v((3, 2, BOTH, 256)), v((3, 2, BOTH, 256)), v((3, 2, BOTH, WW)), v((3, 2, BOTH, WW)),
         v((3, 2, 4, 2, 16, 384)), v((3, 2, 2, 4, 16, 384)),
-        v((16, D), F32), v((16, D), F32), v((16, 128), F32),
+        v((16, D), F32), v((16, 128), F32),
         v((2, FB, QW)), v((2, FB, QW)), v((2, 2, FB, QW)), v((2, 2, FB, QW)),
         v((2, FB, QW), F32),
         v((4, 8, WW), F32), v((2, 8, 8, WW), F32), v((4, 2, 8, WW), F32),
@@ -578,15 +578,14 @@
     return pl.pallas_call(
         body,
         out_shape=(
-            jax.ShapeDtypeStruct((16, D), BF16),
-            jax.ShapeDtypeStruct((TOK, 16), BF16),
-            jax.ShapeDtypeStruct((TOK, 1), F32),
+            jax.ShapeDtypeStruct((32, D), BF16),
+            jax.ShapeDtypeStruct((TOK, 32), BF16),
             jax.ShapeDtypeStruct((1, D), F32),
             jax.ShapeDtypeStruct((QW, FB), BF16),
             jax.ShapeDtypeStruct((FB, QW), BF16),
         ),
         in_specs=[vmem, vmem, hbm, hbm, hbm, hbm],
-        out_specs=(vmem,) * 6,
+        out_specs=(vmem,) * 5,
         scratch_shapes=scratch,
         compiler_params=pltpu.CompilerParams(
             collective_id=0, has_side_effects=True, vmem_limit_bytes=60 * 2**20
@@ -595,10 +594,10 @@
 
 
 def local(tokens, gain, w_up, w_down, cotangent, keep_index):
-    rows, sel, kept, gain_grad, up, down = kernel_call(
+    rows, sel, gain_grad, up, down = kernel_call(
         keep_index, tokens, cotangent, gain.reshape(1, D), w_up, w_down
     )
-    input_grad = jnp.where(kept > 0.5, dot(sel, rows).astype(BF16), cotangent)
+    input_grad = (cotangent.astype(F32) + dot(sel, rows)).astype(BF16)
     return (input_grad, gain_grad.reshape(D), up, down)
 
 

time: 127 us -> 126 us (level)
  no operation moved by 1% of the time
where the time goes in v6:
time: 126 us
  Pallas kernels  119 us (94%)
  matrix products  3.74 us (3%)
  local copies, waits for them, and re-layouts  2.26 us (2%)
    pallas_call x1, Pallas kernels, kernel_call(): pl.pallas_call(body, out_shape=(jax.ShapeDtypeStruct((32, D), BF16), jax....  119 us
    dot_general x1, matrix products, dot(): lax.dot_general(a, b, (((ca,), (cb,)), ((), ())), preferred_element_type=...  3.74 us

profile of v6, /device:TPU:1, one launch (start us, length us, event | category | flops | bytes accessed | tf_op | source)
XLA Modules:
  0.0 126.0 jit_solution(12888561749410443428)
XLA Ops:
  0.6 0.0 copy-start
  0.6 119.4 %shard_map.93 = (bf16[32,6144]{1,0:T(8,128)(2,1)}, bf16[256,32]{1,0:T(8,128)(2,1)}, f32[1,6144]{1,0:T(1,128)}, bf16[768,384]{1,0:T(8,128)(2,1)}, bf16[384,768]{1,0:T(8,128)(2,1)}) custom-call(s32[4,72]{1,0:T(4,128)} %keep_ref.1, f32[1,6144]{1,0:T(1,128)} %bitcast.4, bf16[256,6144]{1,0:T(8,128)(2,1)} %tok_hbm.1, bf16[256,6144]{1,0:T(8,128)(2,1)} %cot_hbm.1, ...), custom_call_target="tpu_custom_call" | custom-call | tf_op jit(solution)/shard_map/pallas_call | solution.py:578
  120.0 0.0 copy-done
  120.0 0.0 copy-start.3
  120.0 0.0 copy-start.2
  120.0 0.0 copy-start.1
  120.0 3.7 %fusion = bf16[256,6144]{1,0:T(8,128)(2,1)} fusion(bf16[256,32]{1,0:T(8,128)(2,1)} %get-tuple-element.9, bf16[32,6144]{1,0:T(8,128)(2,1)} %get-tuple-element.10, bf16[256,6144]{1,0:T(8,128)(2,1)S(1)} %copy-done), kind=kOutput, calls=%fused_computation.1 | convolution fusion | flops 105381888 | bytes 6701056 | tf_op jit(solution)/shard_map/dot_general | solution.py:32
  123.8 0.0 copy-done.3
  123.8 0.6 copy.13
  124.4 0.0 copy-done.2
  124.4 0.8 copy.14
  125.2 0.0 copy-done.1
  125.2 0.8 copy.15
Async XLA Ops:
  0.6 119.4 %copy-start = (bf16[256,6144]{1,0:T(8,128)(2,1)S(1)}, bf16[256,6144]{1,0:T(8,128)(2,1)}, u32[]{:S(2)}) copy-start(bf16[256,6144]{1,0:T(8,128)(2,1)} %cot_hbm.1) | copy-start | bytes 9437188
  120.0 3.8 %copy-start.3 = (f32[1,6144]{1,0:T(1,128)S(1)}, f32[1,6144]{1,0:T(1,128)}, u32[]{:S(2)}) copy-start(f32[1,6144]{1,0:T(1,128)} %get-tuple-element.11) | copy-start | bytes 73732
  120.0 4.4 %copy-start.2 = (bf16[768,384]{1,0:T(8,128)(2,1)S(1)}, bf16[768,384]{1,0:T(8,128)(2,1)}, u32[]{:S(2)}) copy-start(bf16[768,384]{1,0:T(8,128)(2,1)} %get-tuple-element.20) | copy-start | bytes 1769476
  120.0 5.2 %copy-start.1 = (bf16[384,768]{1,0:T(8,128)(2,1)S(1)}, bf16[384,768]{1,0:T(8,128)(2,1)}, u32[]{:S(2)}) copy-start(bf16[384,768]{1,0:T(8,128)(2,1)} %get-tuple-element.21) | copy-start | bytes 1769476

commit v7 on v6

--- a/solution.py
+++ b/solution.py
@@ -316,6 +316,13 @@
         for k in range(3):
             sibs[i, k].wait_recv()
 
+    q_p, q_m, q_2 = step(y, 1), step(y, -1), step(y, 2)
+    q_cols = pl.ds(pl.multiple_of(q_2 * QW, 128), QW)
+
+    def first_terms(s):
+        yield dot(dpre_b[s], t_buf[0, s, :, q_cols], 0, 0)
+        yield dot(act_b[s], t_buf[1, s, :, q_cols], 0, 0)
+
     def far_pair(k):
         fx[2 * k].wait_recv()
         fx[2 * k + 1].wait_recv()
@@ -341,6 +348,7 @@
 
     z_next(5)
     order(4)
+    wd_far = pass_w_down(wd_near)
     order(5)
     pass_on(0)
     pass_on(1)
@@ -350,7 +358,6 @@
     pre_part(0, x)
     pass_on(2)
     pass_on(3)
-    wd_far = pass_w_down(wd_near)
     pass_on(4)
     pass_on(5)
     from_sib(-1)
@@ -369,9 +376,10 @@
     middle(1, s_m)
     far_parts()
     middle(2, s_p)
+    for i, s in enumerate((x, s_m, s_p)):
+        for j, v in enumerate(first_terms(s)):
+            ykeep[j] = v if i == 0 else ykeep[j] + v
     middle(3, s_2)
-
-    dpre_t[...] = dpre_b[...].reshape(4 * BOTH, FB).astype(F32).T.astype(BF16)
 
     def rows_of(a, q):
         v = t_buf[a, :, :, pl.ds(pl.multiple_of(q * QW, 128), QW)]
@@ -384,12 +392,14 @@
         return dot(act_t[...], rows_of(1, q))
 
     yp, ym = y_p, y_m
-    q_p, q_m, q_2 = step(y, 1), step(y, -1), step(y, 2)
-    ys1[0] = up_part(q_2).astype(BF16)
+    terms = first_terms(s_2)
+    ys1[0] = (ykeep[0] + next(terms)).astype(BF16)
     y1u = send(ys1.at[0], yr1.at[0], yp)
+    ys1[1] = (ykeep[1] + next(terms)).astype(BF16)
+    y1d = send(ys1.at[1], yr1.at[1], ym)
+
+    dpre_t[...] = dpre_b[...].reshape(4 * BOTH, FB).astype(F32).T.astype(BF16)
     act_t[...] = act_b[...].reshape(4 * BOTH, FB).astype(F32).T.astype(BF16)
-    ys1[1] = down_part(q_2).astype(BF16)
-    y1d = send(ys1.at[1], yr1.at[1], ym)
 
     gx[pl.ds(x, 1)] = jnp.zeros((1, 8, WW), F32)
     cores, x1, x2, own = {}, {}, {}, {}

time: 126 us -> 131 us (1.040)
  Pallas kernels: 119 us -> 124 us
    pallas_call x1, Pallas kernels: 119 us -> 124 us  [kernel_call(): pl.pallas_call(body, out_shape=(jax.ShapeDtypeStruct((32, D), BF16), jax....]
where the time goes in v7:
time: 131 us
  Pallas kernels  124 us (95%)
  matrix products  3.74 us (3%)
  local copies, waits for them, and re-layouts  2.26 us (2%)
    pallas_call x1, Pallas kernels, kernel_call(): pl.pallas_call(body, out_shape=(jax.ShapeDtypeStruct((32, D), BF16), jax....  124 us
    dot_general x1, matrix products, dot(): lax.dot_general(a, b, (((ca,), (cb,)), ((), ())), preferred_element_type=...  3.74 us

profile of v7, /device:TPU:1, one launch (start us, length us, event | category | flops | bytes accessed | tf_op | source)
XLA Modules:
  0.0 130.7 jit_solution(2590627118135231695)
XLA Ops:
  0.6 0.0 copy-start
  0.6 124.0 %shard_map.93 = (bf16[32,6144]{1,0:T(8,128)(2,1)}, bf16[256,32]{1,0:T(8,128)(2,1)}, f32[1,6144]{1,0:T(1,128)}, bf16[768,384]{1,0:T(8,128)(2,1)}, bf16[384,768]{1,0:T(8,128)(2,1)}) custom-call(s32[4,72]{1,0:T(4,128)} %keep_ref.1, f32[1,6144]{1,0:T(1,128)} %bitcast.4, bf16[256,6144]{1,0:T(8,128)(2,1)} %tok_hbm.1, bf16[256,6144]{1,0:T(8,128)(2,1)} %cot_hbm.1, ...), custom_call_target="tpu_custom_call" | custom-call | tf_op jit(solution)/shard_map/pallas_call | solution.py:588
  124.7 0.0 copy-done
  124.7 0.0 copy-start.3
  124.7 0.0 copy-start.2
  124.7 0.0 copy-start.1
  124.7 3.7 %fusion = bf16[256,6144]{1,0:T(8,128)(2,1)} fusion(bf16[256,32]{1,0:T(8,128)(2,1)} %get-tuple-element.9, bf16[32,6144]{1,0:T(8,128)(2,1)} %get-tuple-element.10, bf16[256,6144]{1,0:T(8,128)(2,1)S(1)} %copy-done), kind=kOutput, calls=%fused_computation.1 | convolution fusion | flops 105381888 | bytes 6701056 | tf_op jit(solution)/shard_map/dot_general | solution.py:32
  128.5 0.0 copy-done.3
  128.5 0.6 copy.13
  129.1 0.0 copy-done.2
  129.1 0.8 copy.14
  129.9 0.0 copy-done.1
  129.9 0.8 copy.15
Async XLA Ops:
  0.6 124.1 %copy-start = (bf16[256,6144]{1,0:T(8,128)(2,1)S(1)}, bf16[256,6144]{1,0:T(8,128)(2,1)}, u32[]{:S(2)}) copy-start(bf16[256,6144]{1,0:T(8,128)(2,1)} %cot_hbm.1) | copy-start | bytes 9437188
  124.7 3.8 %copy-start.3 = (f32[1,6144]{1,0:T(1,128)S(1)}, f32[1,6144]{1,0:T(1,128)}, u32[]{:S(2)}) copy-start(f32[1,6144]{1,0:T(1,128)} %get-tuple-element.11) | copy-start | bytes 73732
  124.7 4.4 %copy-start.2 = (bf16[768,384]{1,0:T(8,128)(2,1)S(1)}, bf16[768,384]{1,0:T(8,128)(2,1)}, u32[]{:S(2)}) copy-start(bf16[768,384]{1,0:T(8,128)(2,1)} %get-tuple-element.20) | copy-start | bytes 1769476
  124.7 5.2 %copy-start.1 = (bf16[384,768]{1,0:T(8,128)(2,1)S(1)}, bf16[384,768]{1,0:T(8,128)(2,1)}, u32[]{:S(2)}) copy-start(bf16[384,768]{1,0:T(8,128)(2,1)} %get-tuple-element.21) | copy-start | bytes 1769476

commit v8 on v7

--- a/solution.py
+++ b/solution.py
@@ -156,6 +156,7 @@
     wu_in.wait()
     wu_r, wu_l = send(wu_own, wu_own, y_p), send(wu_own, wu_own, y_m)
     wd_in.wait()
+    wd_near = send(wd_own, wd_own, y_p), send(wd_own, wd_own, y_m)
 
     def pass_w_up():
         wu_r.wait_recv()
@@ -164,9 +165,6 @@
         wu_l.wait_recv()
         p = wu.at[pl.ds(pl.multiple_of(step(y, 1) * QW + QW // 2, QW // 2), QW // 2)]
         return a, send(p, p, y_m)
-
-    def send_w_down():
-        return send(wd_own, wd_own, y_p), send(wd_own, wd_own, y_m)
 
     def pass_w_down(own):
         own[0].wait_recv()
@@ -334,7 +332,6 @@
     z_own(2)
     z_next(1)
     wu_far = pass_w_up()
-    wd_near = send_w_down()
     order(0)
     z_own(3)
     z_next(2)
@@ -348,8 +345,8 @@
 
     z_next(5)
     order(4)
+    order(5)
     wd_far = pass_w_down(wd_near)
-    order(5)
     pass_on(0)
     pass_on(1)
     for d in wu_far:

time: 131 us -> 126 us (0.962)
  Pallas kernels: 124 us -> 119 us
    pallas_call x1, Pallas kernels: 124 us -> 119 us  [kernel_call(): pl.pallas_call(body, out_shape=(jax.ShapeDtypeStruct((32, D), BF16), jax....]
where the time goes in v8:
time: 126 us
  Pallas kernels  119 us (94%)
  matrix products  3.74 us (3%)
  local copies, waits for them, and re-layouts  2.26 us (2%)
    pallas_call x1, Pallas kernels, kernel_call(): pl.pallas_call(body, out_shape=(jax.ShapeDtypeStruct((32, D), BF16), jax....  119 us
    dot_general x1, matrix products, dot(): lax.dot_general(a, b, (((ca,), (cb,)), ((), ())), preferred_element_type=...  3.74 us

profile of v8, /device:TPU:1, one launch (start us, length us, event | category | flops | bytes accessed | tf_op | source)
XLA Modules:
  0.0 125.9 jit_solution(13192650251357048819)
XLA Ops:
  0.6 0.0 copy-start
  0.6 119.3 %shard_map.93 = (bf16[32,6144]{1,0:T(8,128)(2,1)}, bf16[256,32]{1,0:T(8,128)(2,1)}, f32[1,6144]{1,0:T(1,128)}, bf16[768,384]{1,0:T(8,128)(2,1)}, bf16[384,768]{1,0:T(8,128)(2,1)}) custom-call(s32[4,72]{1,0:T(4,128)} %keep_ref.1, f32[1,6144]{1,0:T(1,128)} %bitcast.4, bf16[256,6144]{1,0:T(8,128)(2,1)} %tok_hbm.1, bf16[256,6144]{1,0:T(8,128)(2,1)} %cot_hbm.1, ...), custom_call_target="tpu_custom_call" | custom-call | tf_op jit(solution)/shard_map/pallas_call | solution.py:585
  119.9 0.0 copy-done
  119.9 0.0 copy-start.3
  119.9 0.0 copy-start.2
  119.9 0.0 copy-start.1
  119.9 3.7 %fusion = bf16[256,6144]{1,0:T(8,128)(2,1)} fusion(bf16[256,32]{1,0:T(8,128)(2,1)} %get-tuple-element.9, bf16[32,6144]{1,0:T(8,128)(2,1)} %get-tuple-element.10, bf16[256,6144]{1,0:T(8,128)(2,1)S(1)} %copy-done), kind=kOutput, calls=%fused_computation.1 | convolution fusion | flops 105381888 | bytes 6701056 | tf_op jit(solution)/shard_map/dot_general | solution.py:32
  123.7 0.0 copy-done.3
  123.7 0.6 copy.13
  124.3 0.0 copy-done.2
  124.3 0.8 copy.14
  125.1 0.0 copy-done.1
  125.1 0.8 copy.15
Async XLA Ops:
  0.6 119.3 %copy-start = (bf16[256,6144]{1,0:T(8,128)(2,1)S(1)}, bf16[256,6144]{1,0:T(8,128)(2,1)}, u32[]{:S(2)}) copy-start(bf16[256,6144]{1,0:T(8,128)(2,1)} %cot_hbm.1) | copy-start | bytes 9437188
  119.9 3.8 %copy-start.3 = (f32[1,6144]{1,0:T(1,128)S(1)}, f32[1,6144]{1,0:T(1,128)}, u32[]{:S(2)}) copy-start(f32[1,6144]{1,0:T(1,128)} %get-tuple-element.11) | copy-start | bytes 73732
  119.9 4.4 %copy-start.2 = (bf16[768,384]{1,0:T(8,128)(2,1)S(1)}, bf16[768,384]{1,0:T(8,128)(2,1)}, u32[]{:S(2)}) copy-start(bf16[768,384]{1,0:T(8,128)(2,1)} %get-tuple-element.20) | copy-start | bytes 1769476
  119.9 5.2 %copy-start.1 = (bf16[384,768]{1,0:T(8,128)(2,1)S(1)}, bf16[384,768]{1,0:T(8,128)(2,1)}, u32[]{:S(2)}) copy-start(bf16[384,768]{1,0:T(8,128)(2,1)} %get-tuple-element.21) | copy-start | bytes 1769476
